TPU v7x, 32 devices: a whole 2x2x4 slice. The times are simulated.
32 devices in a mesh: row: 2 (over core), col: 16 (over z, y, x).
Axes of the slice: x: 2, y: 2, z: 4, core: 2. Of those that a mesh axis runs over, the one named last changes fastest.
Arguments:
- image: bfloat16 [32, 512, 768], P('row', 'col'), may hold values from -6 to 6
- dw_kernel: float32 [768, 49], replicated, may hold values from -0.875 to 0.875
- ln_gain: float32 [768], replicated, may hold values from 0.25 to 1.75
- w_in: bfloat16 [768, 3072], P('col'), may hold values from -0.21875 to 0.21875
- b_in: float32 [3072], replicated, may hold values from -3 to 3
- w_out: bfloat16 [3072, 768], P('col'), may hold values from -0.109375 to 0.109375
- layer_scale: float32 [768], replicated, may hold values from 0.5 to 1.5
- cotangent: bfloat16 [32, 512, 768], P('row', 'col'), may hold values from -8 to 8
Outputs:
- out_map: bfloat16 [32, 512, 768], P('row', 'col')
- grad_image: bfloat16 [32, 512, 768], P('row', 'col')
- grad_kernel: float32 [768, 49], P(('row', 'col'))
- grad_w_in: float32 [768, 3072], P('col')
- grad_w_out: float32 [3072, 768], P('col')
- grad_b_in: float32 [3072], replicated
- grad_gain: float32 [768], replicated
- grad_scale: float32 [768], replicated
All inputs are finite; a program needn't handle non-finite values.
Results may differ from a plain program's by a relative error of at most 0.0071.
Values may be sent and summed in bfloat16 or wider, within the bound.
A program may use at most 128 MiB of HBM per device.

v0:
```python
import math

import jax
import jax.numpy as jnp
from jax import lax
from jax.sharding import PartitionSpec as P

KSIZE = 7
DILATE = 2
REACH = 6


EPSILON = 1e-06
CONTRACT_ROWS = (((0,), (0,)), ((), ()))
CONTRACT_COLS = (((1,), (1,)), ((), ()))


def normal_cdf(values):
    return 0.5 * (1.0 + jax.scipy.special.erf(values * 0.7071067811865476))


def gelu_exact(values):
    return values * normal_cdf(values)


def gelu_slope(values):
    return normal_cdf(values) + values * jnp.exp(-0.5 * values * values) * 0.3989422804014327


def group_stencil(padded, tap_table, height, breadth):
    summed = jnp.zeros((tap_table.shape[0], height, breadth), jnp.float32)
    for tap_row in range(KSIZE):
        for tap_col in range(KSIZE):
            window = padded[
                :,
                DILATE * tap_row : DILATE * tap_row + height,
                DILATE * tap_col : DILATE * tap_col + breadth,
            ].astype(jnp.float32)
            summed = summed + tap_table[:, KSIZE * tap_row + tap_col][:, None, None] * window
    return summed


def group_taps(padded, gradient, height, breadth):
    columns = []
    for tap_row in range(KSIZE):
        for tap_col in range(KSIZE):
            window = padded[
                :,
                DILATE * tap_row : DILATE * tap_row + height,
                DILATE * tap_col : DILATE * tap_col + breadth,
            ].astype(jnp.float32)
            columns.append(jnp.sum(gradient * window, axis=(1, 2)))
    return jnp.stack(columns, axis=1)


def pad_groups(field):
    return jnp.pad(field, ((0, 0), (REACH, REACH), (REACH, REACH)))


def to_groups(field, row_count, col_count):
    tile_rows, tile_cols, channels = field.shape
    group_size = channels // (row_count * col_count)
    pixels = tile_rows * tile_cols
    packed = field.reshape(pixels, channels).T.reshape(row_count, col_count, group_size, pixels)
    moved = lax.all_to_all(
        packed.reshape(row_count * col_count, group_size, pixels),
        ("row", "col"),
        split_axis=0,
        concat_axis=0,
        tiled=True,
    ).reshape(row_count, col_count, group_size, pixels)
    moved = moved.reshape(row_count, col_count, group_size, tile_rows, tile_cols)
    return moved.transpose(2, 0, 3, 1, 4).reshape(
        group_size, row_count * tile_rows, col_count * tile_cols
    )


def from_groups(field, row_count, col_count, tile_rows, tile_cols):
    group_size = field.shape[0]
    pixels = tile_rows * tile_cols
    channels = group_size * row_count * col_count
    packed = field.reshape(group_size, row_count, tile_rows, col_count, tile_cols).transpose(
        1, 3, 0, 2, 4
    )
    packed = packed.reshape(row_count, col_count, group_size, pixels)
    moved = lax.all_to_all(
        packed.reshape(row_count * col_count, group_size, pixels),
        ("row", "col"),
        split_axis=0,
        concat_axis=0,
        tiled=True,
    )
    return moved.reshape(channels, pixels).T.reshape(tile_rows, tile_cols, channels)


def local(image, dw_kernel, ln_gain, w_in, b_in, w_out, layer_scale, cotangent):
    tile_rows, tile_cols, channels = image.shape
    row_count = lax.axis_size("row")
    col_count = lax.axis_size("col")
    group_count = row_count * col_count
    group_size = channels // group_count
    pixels = tile_rows * tile_cols
    scale_factor = 1.0 / math.sqrt(pixels * group_count)
    full_in, full_out = (
        lax.all_gather(w_in, "col", axis=0, tiled=True),
        lax.all_gather(w_out, "col", axis=0, tiled=True),
    )
    flipped = dw_kernel.reshape(channels, KSIZE, KSIZE)[:, ::-1, ::-1].reshape(
        channels, KSIZE * KSIZE
    )
    group_index = lax.axis_index("row") * col_count + lax.axis_index("col")
    kernel_mine = lax.dynamic_slice_in_dim(dw_kernel, group_index * group_size, group_size, 0)
    flipped_mine = lax.dynamic_slice_in_dim(flipped, group_index * group_size, group_size, 0)
    grouped = pad_groups(to_groups(image, row_count, col_count))
    height = grouped.shape[1] - 2 * REACH
    breadth = grouped.shape[2] - 2 * REACH
    conv_groups = group_stencil(grouped, kernel_mine, height, breadth).astype(jnp.bfloat16)
    conv_tile = from_groups(conv_groups, row_count, col_count, tile_rows, tile_cols)
    conv_rows = conv_tile.astype(jnp.float32).reshape(pixels, channels)
    average = jnp.mean(conv_rows, axis=1, keepdims=True)
    centered = conv_rows - average
    inverse = lax.rsqrt(jnp.mean(centered * centered, axis=1, keepdims=True) + EPSILON)
    standard = centered * inverse
    normed = (standard * ln_gain).astype(jnp.bfloat16)
    preact = jnp.dot(normed, full_in, preferred_element_type=jnp.float32) + b_in
    hidden = gelu_exact(preact).astype(jnp.bfloat16)
    mixed = jnp.dot(hidden, full_out, preferred_element_type=jnp.float32)
    out_map = (image.reshape(pixels, channels).astype(jnp.float32) + layer_scale * mixed).astype(
        jnp.bfloat16
    )
    out_map = out_map.reshape(tile_rows, tile_cols, channels)
    upstream = cotangent.reshape(pixels, channels).astype(jnp.float32)
    scale_part = jnp.sum(upstream * mixed, axis=0)
    grad_mix = (upstream * layer_scale).astype(jnp.bfloat16)
    grad_hidden = lax.dot_general(
        grad_mix, full_out, CONTRACT_COLS, preferred_element_type=jnp.float32
    )
    grad_pre = grad_hidden * gelu_slope(preact)
    bias_part = jnp.sum(grad_pre, axis=0)
    grad_pre_rounded = grad_pre.astype(jnp.bfloat16)
    grad_norm = lax.dot_general(
        grad_pre_rounded, full_in, CONTRACT_COLS, preferred_element_type=jnp.float32
    )
    picked = normed
    part_in = lax.psum_scatter(
        lax.dot_general(
            picked, grad_pre_rounded, CONTRACT_ROWS, preferred_element_type=jnp.float32
        ),
        "col",
        scatter_dimension=0,
        tiled=True,
    )
    picked = hidden
    part_out = lax.psum_scatter(
        lax.dot_general(picked, grad_mix, CONTRACT_ROWS, preferred_element_type=jnp.float32),
        "col",
        scatter_dimension=0,
        tiled=True,
    )
    summed_in, summed_out = lax.psum((part_in, part_out), "row")
    gain_part = jnp.sum(grad_norm * standard, axis=0)
    scaled = grad_norm * ln_gain
    grad_conv = (
        (
            scaled
            - jnp.mean(scaled, axis=1, keepdims=True)
            - standard * jnp.mean(scaled * standard, axis=1, keepdims=True)
        )
        * inverse
    ).astype(jnp.bfloat16)
    grad_conv = grad_conv.reshape(tile_rows, tile_cols, channels)
    grad_groups = to_groups(grad_conv, row_count, col_count)
    back_groups = group_stencil(pad_groups(grad_groups), flipped_mine, height, breadth).astype(
        jnp.bfloat16
    )
    grad_back = from_groups(back_groups, row_count, col_count, tile_rows, tile_cols)
    grad_kernel = (
        group_taps(grouped, grad_groups.astype(jnp.float32), height, breadth) * scale_factor
    )
    grad_image = (cotangent.astype(jnp.float32) + grad_back.astype(jnp.float32)).astype(
        jnp.bfloat16
    )
    scale_sum, bias_sum, gain_sum = lax.psum((scale_part, bias_part, gain_part), ("row", "col"))
    return (
        out_map,
        grad_image,
        grad_kernel,
        summed_in * scale_factor,
        summed_out * scale_factor,
        bias_sum * scale_factor,
        gain_sum * scale_factor,
        scale_sum * scale_factor,
    )


def solution(mesh):
    in_specs = (
        P("row", "col", None),
        P(),
        P(),
        P("col", None),
        P(),
        P("col", None),
        P(),
        P("row", "col", None),
    )
    out_specs = (
        P("row", "col", None),
        P("row", "col", None),
        P(("row", "col"), None),
        P("col", None),
        P("col", None),
        P(),
        P(),
        P(),
    )
    return jax.shard_map(local, mesh=mesh, in_specs=in_specs, out_specs=out_specs, check_vma=False)
```

profile of v0, /device:TPU:0, one launch (start us, length us, event | category | flops | bytes accessed | tf_op | source)
XLA Modules:
  0.0 619.7 jit_solution(1047436947445705504)
XLA Ops:
  7.2 0.7 all-gather.3.cloned.1.call-update
  7.9 0.7 all-gather.5.cloned.1.call-update
  8.7 2.3 copy.33
  11.0 7.4 %all-to-all-start = ((bf16[32,24,512]{2,1,0:T(8,128)(2,1)}), bf16[32,24,512]{2,1,0:T(8,128)(2,1)}, u32[]{:S(2)}, u32[]{:S(2)}) async-start(bf16[32,24,512]{2,1,0:T(8,128)(2,1)} %bitcast.3), calls=%async_computation | async-start | bytes 1572864 | tf_op jit(solution)/shard_map/all_to_all | solution.py:65
  18.5 0.1 dynamic-slice_bitcast_fusion.95
  18.6 0.1 dynamic-slice_bitcast_fusion.96
  18.8 0.1 dynamic-slice_bitcast_fusion.97
  18.9 28.3 %all-to-all-done = bf16[32,24,512]{2,1,0:T(8,128)(2,1)} async-done(((bf16[32,24,512]{2,1,0:T(8,128)(2,1)}), bf16[32,24,512]{2,1,0:T(8,128)(2,1)}, u32[]{:S(2)}, u32[]{:S(2)}) %all-to-all-start) | async-done | bytes 786464 | tf_op jit(solution)/shard_map/all_to_all | solution.py:65
  47.2 3.4 reshape_reshape.19
  50.6 5.3 copy.97
  55.9 5.4 reshape.178
  61.3 47.3 %fusion.139 = bf16[24,32,512]{2,1,0:T(8,128)(2,1)} fusion(bf16[24,32,512]{2,1,0:T(8,128)(2,1)} %reshape.178, f32[24]{0:T(128)S(1)} %get-tuple-element.188, f32[24]{0:T(128)S(1)} %get-tuple-element.141, f32[24]{0:T(128)S(1)} %get-tuple-element.142, f32[24]{0:T(128)S(1)} %get-tuple-element.143, f32[24]{0:T(128)S(1)} %get-tuple-element.144, ...), kind=kLoop, calls=%fused_computation.348 | loop fusion | flops 57802752 | bytes 1577568 | tf_op jit(solution)/shard_map/convert_element_type | solution.py:117
  108.5 4.6 reshape.179
  113.1 4.4 copy.35
  117.5 5.3 reshape_reshape.20
  122.9 38.7 %all_to_all.20 = bf16[32,24,512]{2,1,0:T(8,128)(2,1)} all-to-all(bf16[32,24,512]{2,1,0:T(8,128)(2,1)} %reshape_reshape.20), channel_id=1, replica_groups=mesh['row'=2,'col'=16] {'row','col'}, dimensions={0} | all-to-all | bytes 1572864 | tf_op jit(solution)/shard_map/all_to_all | solution.py:86
  161.6 2.6 copy.36
  164.2 1.3 convert_reduce_fusion
  165.5 1.7 multiply_reduce_fusion.1
  167.3 8.6 %multiply_convert_fusion = (bf16[512,3072]{1,0:T(8,128)(2,1)}, f32[512,3072]{1,0:T(8,128)}) fusion(f32[3072]{0:T(1024)S(1)} %copy-done.10, bf16[768,3072]{1,0:T(8,128)(2,1)} %all-gather.3.cloned.1.call-done, f32[768,512]{0,1:T(8,128)} %copy.36, f32[768]{0:T(1024)S(1)} %copy-done.7, f32[512]{0:T(512)S(1)} %add_rsqrt_fusion, f32[512]{0:T(512)S(1)} %broadcast_multiply_fusion.8), kind=kOutput, calls=%fused_computation.152 | convolution fusion | flops 2426929152 | bytes 15748096 | tf_op jit(solution)/shard_map/dot_general | solution.py:125
  175.9 17.7 %all-gather.5.cloned.1.call-done = bf16[3072,768]{1,0:T(8,128)(2,1)} async-done(((bf16[192,768]{1,0:T(8,128)(2,1)}), bf16[3072,768]{1,0:T(8,128)(2,1)}) %all-gather.5.cloned.1.call-update) | async-done | bytes 4718608 | tf_op jit(solution)/shard_map/all_gather | solution.py:106
  193.7 7.4 %fusion.130 = (f32[768]{0:T(1024)S(1)}, bf16[512,768]{1,0:T(8,128)(2,1)}, bf16[512,768]{1,0:T(8,128)(2,1)S(1)}) fusion(bf16[16,32,768]{2,1,0:T(8,128)(2,1)} %param.15, f32[768]{0:T(1024)S(1)} %copy-done.11, bf16[16,32,768]{2,1,0:T(8,128)(2,1)} %param.8, bf16[512,3072]{1,0:T(8,128)(2,1)} %get-tuple-element.189, ...), kind=kOutput, calls=%fused_computation.334 | convolution fusion | flops 2419457280 | bytes 11016192 | tf_op jit(solution)/shard_map/dot_general | solution.py:127
  201.1 4.7 fusion.143
  205.8 1.7 copy-done.4
  207.5 5.5 fusion.134
  213.0 0.5 reduce-scatter.5.cloned.1.call-start
  213.5 8.4 %fusion.144 = f32[3072,768]{1,0:T(8,128)} fusion(bf16[512,3072]{1,0:T(8,128)(2,1)} %get-tuple-element.189, bf16[512,768]{1,0:T(8,128)(2,1)} %copy-done.12), kind=kOutput, calls=%fused_computation.462 | convolution fusion | flops 2415919104 | bytes 13369344 | tf_op jit(solution)/shard_map/dot_general | solution.py:155
  221.9 6.8 %fusion.133 = (f32[768]{0:T(1024)S(1)}, f32[512]{0:T(512)S(1)}, f32[512]{0:T(512)S(1)}, f32[512,768]{1,0:T(8,128)S(1)}) fusion(f32[768,512]{0,1:T(8,128)} %copy.36, f32[512]{0:T(512)S(1)} %add_rsqrt_fusion, f32[512]{0:T(512)S(1)} %broadcast_multiply_fusion.8, f32[768]{0:T(1024)S(1)} %copy-done.7, bf16[768,3072]{1,0:T(8,128)(2,1)} %all-gather.3.cloned.1.call-done, ...), kind=kOutput, calls=%fused_computation.340 | convolution fusion | flops 2419063040 | bytes 11024384 | tf_op jit(solution)/shard_map/dot_general | solution.py:141
  228.7 1.3 fusion.127
  230.0 2.3 copy.37
  232.4 3.3 all-to-all-start.2
  235.8 0.2 rev.3
  236.0 0.1 dynamic-slice_bitcast_fusion.46
  236.2 0.6 dynamic-slice_bitcast_fusion.47
  236.8 0.1 dynamic-slice_bitcast_fusion.48
  237.0 58.5 %all-reduce.2 = (f32[3072]{0:T(1024)S(1)}, f32[768]{0:T(1024)S(1)}, f32[768]{0:T(1024)S(1)}) all-reduce(f32[3072]{0:T(1024)S(1)} %get-tuple-element.192, f32[768]{0:T(1024)S(1)} %get-tuple-element.32, f32[768]{0:T(1024)S(1)} %get-tuple-element.88), channel_id=1, replica_groups=mesh['row'=2,'col'=16] {'row','col'}, use_global_device_ids=true, to_apply=%region_58.59 | all-reduce | flops 4608 | bytes 36864 | tf_op jit(solution)/shard_map/psum | solution.py:183
  295.4 0.6 broadcast_multiply_fusion.4
  296.0 0.6 broadcast_multiply_fusion.2
  296.6 4.6 reshape_reshape.22
  301.2 7.2 %copy.96 = bf16[2,16,24,16,32]{4,1,3,0,2:T(8,128)(2,1)} copy(bf16[2,16,24,16,32]{4,3,2,1,0:T(8,128)(2,1)} %reshape_reshape.22) | data formatting | bytes 1572864 | tf_op jit(solution)/shard_map/reshape;reshape | solution.py:72
  308.5 5.4 reshape.183
  313.8 45.7 %fusion.138 = bf16[24,32,512]{2,1,0:T(8,128)(2,1)} fusion(bf16[24,32,512]{2,1,0:T(8,128)(2,1)} %reshape.183, f32[24]{0:T(128)S(1)} %get-tuple-element.139, f32[24]{0:T(128)S(1)} %get-tuple-element.92, f32[24]{0:T(128)S(1)} %get-tuple-element.93, f32[24]{0:T(128)S(1)} %get-tuple-element.94, f32[24]{0:T(128)S(1)} %get-tuple-element.95, ...), kind=kLoop, calls=%fused_computation.347 | loop fusion | flops 57802752 | bytes 1577568 | tf_op jit(solution)/shard_map/convert_element_type | solution.py:173
  359.5 4.6 reshape.184
  364.1 4.5 copy.39
  368.6 5.4 reshape_reshape.23
  374.0 4.4 all-to-all-start.3
  378.5 18.7 %fusion.124 = (f32[24]{0:T(128)S(1)}, f32[24]{0:T(128)S(1)}, f32[24]{0:T(128)S(1)}, f32[24]{0:T(128)S(1)}, f32[24]{0:T(128)S(1)}, /*index=5*/f32[24]{0:T(128)S(1...) fusion(bf16[24,32,512]{2,1,0:T(8,128)(2,1)} %reshape.183, ...), kind=kLoop, calls=%fused_computation.323 | loop fusion | flops 21626448 | bytes 1574592 | tf_op jit(solution)/shard_map/reduce_sum | solution.py:52
  397.2 7.3 %fusion.125 = (f32[24]{0:T(128)S(1)}, f32[24]{0:T(128)S(1)}, f32[24]{0:T(128)S(1)}, f32[24]{0:T(128)S(1)}, f32[24]{0:T(128)S(1)}, /*index=5*/f32[24]{0:T(128)S(1...) fusion(bf16[24,32,512]{2,1,0:T(8,128)(2,1)S(1)} %copy-done.3, ...), kind=kLoop, calls=%fused_computation.324 | loop fusion | flops 21626448 | bytes 1574592 | tf_op jit(solution)/shard_map/reduce_sum | solution.py:52
  404.5 0.1 copy.59
  404.6 0.1 copy.88
  404.7 0.1 copy.42
  404.9 14.7 %fusion.123 = (f32[24]{0:T(128)S(1)}, f32[24]{0:T(128)S(1)}, f32[24]{0:T(128)S(1)}, f32[24]{0:T(128)S(1)}, f32[24]{0:T(128)S(1)}, /*index=5*/f32[24]{0:T(128)S(1...) fusion(bf16[24,32,512]{2,1,0:T(8,128)(2,1)} %reshape.183, ...), kind=kLoop, calls=%fused_computation.322 | loop fusion | flops 14548704 | bytes 1574016 | tf_op jit(solution)/shard_map/reduce_sum | solution.py:52
  419.6 0.1 copy.77
  419.7 168.9 %reduce-scatter.5.cloned.1.call-done = f32[192,768]{1,0:T(8,128)} async-done(((f32[3072,768]{1,0:T(8,128)}), f32[192,768]{1,0:T(8,128)}) %reduce-scatter.5.cloned.1.call-update) | async-done | bytes 589840 | tf_op jit(solution)/shard_map/reduce_scatter | solution.py:154
  588.6 5.6 multiply_reduce_fusion
  594.2 0.1 copy.65
  597.9 0.2 stack.199
  598.1 0.6 broadcast_multiply_fusion.3
  598.7 1.3 convert_bitcast_fusion
  600.0 0.5 copy.40
  600.5 2.2 fusion.128
  602.7 7.1 %all-reduce.6.cloned.1.call-done = (f32[48,3072]{1,0:T(8,128)}, f32[192,768]{1,0:T(8,128)}) async-done(((f32[48,3072]{1,0:T(8,128)}, f32[192,768]{1,0:T(8,128)}), (f32[48,3072]{1,0:T(8,128)}, f32[192,768]{1,0:T(8,128)})) %all-reduce.6.cloned.1.call-update) | async-done | bytes 1179664 | tf_op jit(solution)/shard_map/psum | solution.py:160
  609.8 2.0 broadcast_multiply_fusion.1
  611.8 0.9 broadcast_multiply_fusion
  (87 shorter events, 4.1 us)
Async XLA Ops:
  7.2 160.1 %all-gather.3.cloned.1.call-start = ((), (), s32[]{:S(2)}) async-start(), calls=%async_computation.6 | async-start | bytes 5013504 | tf_op jit(solution)/shard_map/all_gather | solution.py:105
  7.9 185.7 %all-gather.5.cloned.1.call-start = ((), (), s32[]{:S(2)}) async-start(), calls=%async_computation.7 | async-start | bytes 5013504 | tf_op jit(solution)/shard_map/all_gather | solution.py:106
  8.7 9.8 %copy-start.6 = (f32[768,49]{0,1:T(8,128)S(1)}, f32[768,49]{0,1:T(8,128)}, u32[]{:S(2)}) copy-start(f32[768,49]{0,1:T(8,128)} %param.9) | copy-start | bytes 451588
  11.0 36.2 %all-to-all-start = ((bf16[32,24,512]{2,1,0:T(8,128)(2,1)}), bf16[32,24,512]{2,1,0:T(8,128)(2,1)}, u32[]{:S(2)}, u32[]{:S(2)}) async-start(bf16[32,24,512]{2,1,0:T(8,128)(2,1)} %bitcast.3), calls=%async_computation | async-start | bytes 1572864 | tf_op jit(solution)/shard_map/all_to_all | solution.py:65
  18.4 401.3 %reduce-scatter.3.cloned.1.call-start = ((), (), s32[]{:S(2)}) async-start(), calls=%async_computation.8 | async-start | bytes 10027008 | tf_op jit(solution)/shard_map/reduce_scatter | solution.py:145
  164.2 3.1 copy-start.7
  164.2 3.1 copy-start.10
  167.2 26.4 %copy-start.11 = (f32[768]{0:T(1024)S(1)}, f32[768]{0:T(1024)}, u32[]{:S(2)}) copy-start(f32[768]{0:T(1024)} %param.14) | copy-start | bytes 9220
  193.6 7.4 %copy-start.9 = (bf16[3072,768]{1,0:T(8,128)(2,1)S(1)}, bf16[3072,768]{1,0:T(8,128)(2,1)}, u32[]{:S(2)}) copy-start(bf16[3072,768]{1,0:T(8,128)(2,1)} %all-gather.5.cloned.1.call-done) | copy-start | bytes 14155780
  193.7 7.4 %copy-start.13 = (f32[512,3072]{1,0:T(8,128)S(1)}, f32[512,3072]{1,0:T(8,128)}, u32[]{:S(2)}) copy-start(f32[512,3072]{1,0:T(8,128)} %get-tuple-element.190) | copy-start | bytes 18874372
  201.1 4.7 copy-start.12
  201.1 6.4 %copy-start = (f32[768,512]{0,1:T(8,128)S(1)}, f32[768,512]{0,1:T(8,128)}, u32[]{:S(2)}) copy-start(f32[768,512]{0,1:T(8,128)} %copy.36) | copy-start | bytes 4718596
  205.8 1.7 copy-start.4
  213.0 375.7 %reduce-scatter.5.cloned.1.call-start = ((), (), s32[]{:S(2)}) async-start(), calls=%async_computation.9 | async-start | bytes 10027008 | tf_op jit(solution)/shard_map/reduce_scatter | solution.py:154
  221.9 6.8 %copy-start.1 = (f32[768,512]{0,1:T(8,128)S(1)}, f32[768,512]{0,1:T(8,128)}, u32[]{:S(2)}) copy-start(f32[768,512]{0,1:T(8,128)} %copy.36) | copy-start | bytes 4718596
  232.4 64.2 %all-to-all-start.2 = ((bf16[32,24,512]{2,1,0:T(8,128)(2,1)}), bf16[32,24,512]{2,1,0:T(8,128)(2,1)}, u32[]{:S(2)}, u32[]{:S(2)}) async-start(bf16[32,24,512]{2,1,0:T(8,128)(2,1)} %bitcast.327), calls=%async_computation.2 | async-start | bytes 1572864 | tf_op jit(solution)/shard_map/all_to_all | solution.py:65
  308.5 5.4 copy-start.8
  374.0 224.7 %all-to-all-start.3 = ((bf16[32,24,512]{2,1,0:T(8,128)(2,1)}), bf16[32,24,512]{2,1,0:T(8,128)(2,1)}, u32[]{:S(2)}, u32[]{:S(2)}) async-start(bf16[32,24,512]{2,1,0:T(8,128)(2,1)} %reshape_reshape.23), calls=%async_computation.3 | async-start | bytes 1572864 | tf_op jit(solution)/shard_map/all_to_all | solution.py:86
  378.4 231.4 %all-reduce.6.cloned.1.call-start = ((), (), s32[]{:S(2)}) async-start(), calls=%async_computation.10 | async-start | bytes 2359296 | tf_op jit(solution)/shard_map/psum | solution.py:160
  378.5 18.7 %copy-start.2 = (bf16[24,32,512]{2,1,0:T(8,128)(2,1)S(1)}, bf16[24,32,512]{2,1,0:T(8,128)(2,1)}, u32[]{:S(2)}) copy-start(bf16[24,32,512]{2,1,0:T(8,128)(2,1)} %reshape.178) | copy-start | bytes 2359300
  378.5 18.7 %copy-start.3 = (bf16[24,32,512]{2,1,0:T(8,128)(2,1)S(1)}, bf16[24,32,512]{2,1,0:T(8,128)(2,1)}, u32[]{:S(2)}) copy-start(bf16[24,32,512]{2,1,0:T(8,128)(2,1)} %reshape.183) | copy-start | bytes 2359300
  609.8 2.0 copy-start.5
Sparse Core Ops, SparseCore 0:
  10.8 88.8 all-gather.2
  102.5 91.1 all-gather.4
  213.1 199.2 reduce-scatter.2
  418.8 169.7 reduce-scatter.4
  590.8 18.9 all-reduce.5
where the time goes:
time: 627 us; the launch traced here: 620 us
  waiting for transfers between devices  223 us (36%)
  other arithmetic  152 us (24%)
  blocking collectives  97.1 us (15%)
  local copies, waits for them, and re-layouts  75.7 us (12%)
  matrix products  41.3 us (7%)
  starting transfers between devices  15.8 us (3%)
  between operations  14.6 us (2%)
    reduce_scatter x1, waiting for transfers between devices, local(): lax.psum_scatter(lax.dot_general(picked, grad_mix, CONTRACT_ROWS, preferr...  169 us
    psum x1, blocking collectives, local(): lax.psum((scale_part, bias_part, gain_part), ('row', 'col'))  58.5 us
    convert_element_type x1, other arithmetic, local(): group_stencil(grouped, kernel_mine, height, breadth).astype(jnp.bfloat16)  47.3 us
    reduce_sum x4, other arithmetic, group_taps(): columns.append(jnp.sum(gradient * window, axis=(1, 2)))  46.2 us
    convert_element_type x1, other arithmetic, local(): group_stencil(pad_groups(grad_groups), flipped_mine, height, breadth)  45.7 us
    all_to_all x1, blocking collectives, from_groups(): lax.all_to_all(packed.reshape(row_count * col_count, group_size, pixels),...  38.7 us
    all_to_all x2, waiting for transfers between devices, to_groups(): lax.all_to_all(packed.reshape(row_count * col_count, group_size, pixels),...  28.3 us
    another operation x4, local copies, waits for them, and re-layouts, to_groups(): moved.reshape(row_count, col_count, group_size, tile_rows, tile_cols)  20.6 us
  transfers between devices with their start and end apart: 8, of which 4 were waited for; matrix products, arithmetic and copies ran while one was open for 40% of the time, Pallas kernels for 0%

commit v1 on v0

v1 whole, which is shorter than its diff:
```python
import functools
import math

import jax
import jax.numpy as jnp
from jax import lax
from jax.experimental import pallas as pl
from jax.experimental.pallas import tpu as pltpu
from jax.sharding import PartitionSpec as P

KSIZE = 7
TAPS = KSIZE * KSIZE
DILATE = 2
REACH = 6
LANES = 128
PHASES = 4
EPSILON = 1e-06
VMEM_BYTES = 56 * 1024 * 1024
CONTRACT_ROWS = (((0,), (0,)), ((), ()))
CONTRACT_COLS = (((1,), (1,)), ((), ()))


def dot(left, right, dims=(((1,), (0,)), ((), ()))):
    return lax.dot_general(left, right, dims, preferred_element_type=jnp.float32)


def halo_pad(tile):
    cols = lax.axis_size("col")
    rows = lax.axis_size("row")
    ahead = lambda n: [(i, i + 1) for i in range(n - 1)]
    back = lambda n: [(i + 1, i) for i in range(n - 1)]
    left = lax.ppermute(tile[:, -REACH:], "col", ahead(cols))
    right = lax.ppermute(tile[:, :REACH], "col", back(cols))
    wide = jnp.concatenate([left, tile, right], axis=1)
    top = lax.ppermute(wide[-REACH:], "row", ahead(rows))
    bottom = lax.ppermute(wide[:REACH], "row", back(rows))
    return jnp.concatenate([top, wide, bottom], axis=0)


def spread(source, flat, phased, phase_count):
    flat[...] = source[...].astype(jnp.float32)

    def one_row(row, carry):
        for phase in range(phase_count):
            phased[row, phase] = flat[row, pl.ds(phase, 8, stride=PHASES), :]
        return carry

    lax.fori_loop(0, source.shape[0], one_row, 0)


def stencil_blocks(taps_ref, phased, summed, half_rows):
    def block(index, carry):
        parity = lax.rem(index, 2)
        phase = lax.div(index, 2)
        totals = [jnp.zeros((8, LANES), jnp.float32) for _ in range(half_rows)]
        for tap_col in range(KSIZE):
            weights = [
                jnp.broadcast_to(taps_ref[pl.ds(KSIZE * a + tap_col, 1), :], (8, LANES))
                for a in range(KSIZE)
            ]
            for row in range(half_rows + KSIZE - 1):
                window = phased[parity + 2 * row, phase + DILATE * tap_col]
                for a in range(KSIZE):
                    if 0 <= row - a < half_rows:
                        totals[row - a] = totals[row - a] + weights[a] * window
        for row in range(half_rows):
            summed[parity + 2 * row, pl.ds(phase, 8, stride=PHASES), :] = totals[row]
        return carry

    lax.fori_loop(0, 2 * PHASES, block, 0)


def forward_kernel(padded_ref, taps_ref, out_ref, flat, phased, summed):
    spread(padded_ref, flat, phased, 4 * PHASES)
    stencil_blocks(taps_ref, phased, summed, out_ref.shape[0] // 2)
    out_ref[...] = summed[...].astype(jnp.bfloat16)


def backward_kernel(padded_ref, taps_ref, cot_ref, out_ref, flat, phased, summed):
    spread(padded_ref, flat, phased, 4 * PHASES)
    stencil_blocks(taps_ref, phased, summed, out_ref.shape[0] // 2)
    back = summed[...].astype(jnp.bfloat16).astype(jnp.float32)
    out_ref[...] = (cot_ref[...].astype(jnp.float32) + back).astype(jnp.bfloat16)


def taps_kernel(padded_ref, grad_ref, out_ref, flat, phased, grad_flat, grad_phased, totals):
    half_rows = grad_ref.shape[0] // 2
    spread(padded_ref, flat, phased, 4 * PHASES)
    spread(grad_ref, grad_flat, grad_phased, PHASES)
    totals[...] = jnp.zeros_like(totals)

    def block(index, carry):
        parity = lax.rem(index, 2)
        phase = lax.div(index, 2)
        grads = [grad_phased[parity + 2 * row, phase] for row in range(half_rows)]
        for tap_col in range(KSIZE):
            sums = [totals[KSIZE * a + tap_col] for a in range(KSIZE)]
            for row in range(half_rows + KSIZE - 1):
                window = phased[parity + 2 * row, phase + DILATE * tap_col]
                for a in range(KSIZE):
                    if 0 <= row - a < half_rows:
                        sums[a] = sums[a] + grads[row - a] * window
            for a in range(KSIZE):
                totals[KSIZE * a + tap_col] = sums[a]
        return carry

    lax.fori_loop(0, 2 * PHASES, block, 0)
    out_ref[...] = jnp.sum(totals[...], axis=1)


def stencil_cost(rows, cols, channels):
    return pl.CostEstimate(
        flops=2 * TAPS * rows * cols * channels,
        bytes_accessed=8 * rows * cols * channels,
        transcendentals=0,
    )


def stencil_call(kernel, padded, taps, extra, tile_shape):
    rows, cols, channels = tile_shape
    padded_rows, padded_cols, _ = padded.shape
    field = lambda h, w: pl.BlockSpec((h, w, LANES), lambda c: (0, 0, c))
    return pl.pallas_call(
        kernel,
        grid=(channels // LANES,),
        out_shape=jax.ShapeDtypeStruct(tile_shape, jnp.bfloat16),
        in_specs=[
            field(padded_rows, padded_cols),
            pl.BlockSpec((TAPS, LANES), lambda c: (0, c)),
        ]
        + [field(rows, cols)] * len(extra),
        out_specs=field(rows, cols),
        scratch_shapes=[
            pltpu.VMEM((padded_rows, padded_cols, LANES), jnp.float32),
            pltpu.VMEM((padded_rows, 4 * PHASES, 8, LANES), jnp.float32),
            pltpu.VMEM((rows, cols, LANES), jnp.float32),
        ],
        compiler_params=pltpu.CompilerParams(vmem_limit_bytes=VMEM_BYTES),
        cost_estimate=stencil_cost(rows, cols, channels),
    )(padded, taps, *extra)


def taps_call(padded, grad):
    rows, cols, channels = grad.shape
    padded_rows, padded_cols, _ = padded.shape
    field = lambda h, w: pl.BlockSpec((h, w, LANES), lambda c: (0, 0, c))
    return pl.pallas_call(
        taps_kernel,
        grid=(channels // LANES,),
        out_shape=jax.ShapeDtypeStruct((TAPS, channels), jnp.float32),
        in_specs=[field(padded_rows, padded_cols), field(rows, cols)],
        out_specs=pl.BlockSpec((TAPS, LANES), lambda c: (0, c)),
        scratch_shapes=[
            pltpu.VMEM((padded_rows, padded_cols, LANES), jnp.float32),
            pltpu.VMEM((padded_rows, 4 * PHASES, 8, LANES), jnp.float32),
            pltpu.VMEM((rows, cols, LANES), jnp.float32),
            pltpu.VMEM((rows, PHASES, 8, LANES), jnp.float32),
            pltpu.VMEM((TAPS, 8, LANES), jnp.float32),
        ],
        compiler_params=pltpu.CompilerParams(vmem_limit_bytes=VMEM_BYTES),
        cost_estimate=stencil_cost(rows, cols, channels),
    )(padded, grad)


def standardize(conv):
    values = conv.astype(jnp.float32)
    centered = values - jnp.mean(values, axis=1, keepdims=True)
    inverse = lax.rsqrt(jnp.mean(centered * centered, axis=1, keepdims=True) + EPSILON)
    return centered * inverse, inverse


ROW_TILE = 128


def mlp_kernel(
    conv_ref, image_ref, cot_ref, gain_ref, layer_ref, bias_ref, w_in_ref, w_out_ref,
    out_ref, grad_conv_ref, grad_in_ref, grad_out_ref, bias_sum_ref, gain_sum_ref, scale_sum_ref,
    normed, normed_t, grad_mix, mixed, grad_norm, hidden, grad_pre,
):
    step = pl.program_id(0)
    pixels = normed.shape[0]
    tiles = [pl.ds(start, ROW_TILE) for start in range(0, pixels, ROW_TILE)]

    @pl.when(step == 0)
    def _():
        for tile in tiles:
            standard, _ = standardize(conv_ref[tile, :])
            rounded = (standard * gain_ref[...]).astype(jnp.bfloat16)
            normed[tile, :] = rounded
            normed_t[:, tile] = rounded.T
            grad_mix[tile, :] = (cot_ref[tile, :].astype(jnp.float32) * layer_ref[...]).astype(
                jnp.bfloat16
            )
        mixed[...] = jnp.zeros_like(mixed)
        grad_norm[...] = jnp.zeros_like(grad_norm)

    bias_total = jnp.zeros(bias_sum_ref.shape, jnp.float32)
    for tile in tiles:
        preact = dot(normed[tile, :], w_in_ref[...]) + bias_ref[...]
        grad_hidden = dot(grad_mix[tile, :], w_out_ref[...], CONTRACT_COLS)
        cdf = 0.5 * (1.0 + lax.erf(preact * 0.7071067811865476))
        slope = cdf + preact * jnp.exp(-0.5 * preact * preact) * 0.3989422804014327
        grad_value = grad_hidden * slope
        bias_total = bias_total + jnp.sum(grad_value, axis=0, keepdims=True)
        hidden_tile = (preact * cdf).astype(jnp.bfloat16)
        pre_tile = grad_value.astype(jnp.bfloat16)
        hidden[tile, :] = hidden_tile
        grad_pre[tile, :] = pre_tile
        mixed[tile, :] += dot(hidden_tile, w_out_ref[...])
        grad_norm[tile, :] += dot(pre_tile, w_in_ref[...], CONTRACT_COLS)
    bias_sum_ref[...] = bias_total
    grad_in_ref[...] = dot(normed_t[...], grad_pre[...]).astype(grad_in_ref.dtype)
    grad_out_ref[...] = dot(hidden[...], grad_mix[...], CONTRACT_ROWS).astype(grad_out_ref.dtype)

    @pl.when(step == pl.num_programs(0) - 1)
    def _():
        gain_total = jnp.zeros(gain_sum_ref.shape, jnp.float32)
        scale_total = jnp.zeros(scale_sum_ref.shape, jnp.float32)
        for tile in tiles:
            mix = mixed[tile, :]
            out_ref[tile, :] = (
                image_ref[tile, :].astype(jnp.float32) + layer_ref[...] * mix
            ).astype(jnp.bfloat16)
            scale_total = scale_total + jnp.sum(
                cot_ref[tile, :].astype(jnp.float32) * mix, axis=0, keepdims=True
            )
            standard, inverse = standardize(conv_ref[tile, :])
            grad = grad_norm[tile, :]
            gain_total = gain_total + jnp.sum(grad * standard, axis=0, keepdims=True)
            scaled = grad * gain_ref[...]
            grad_conv_ref[tile, :] = (
                (
                    scaled
                    - jnp.mean(scaled, axis=1, keepdims=True)
                    - standard * jnp.mean(scaled * standard, axis=1, keepdims=True)
                )
                * inverse
            ).astype(jnp.bfloat16)
        gain_sum_ref[...] = gain_total
        scale_sum_ref[...] = scale_total


def mlp_call(conv, image, cot, gain, layer, bias, w_in, w_out, grad_type, chunk=256):
    pixels, channels = conv.shape
    hidden_units = w_in.shape[1]
    whole = lambda h, w: pl.BlockSpec((h, w), lambda s: (0, 0))
    f32 = lambda *shape: jax.ShapeDtypeStruct(shape, jnp.float32)
    bf16 = lambda *shape: jax.ShapeDtypeStruct(shape, jnp.bfloat16)
    return pl.pallas_call(
        mlp_kernel,
        grid=(hidden_units // chunk,),
        out_shape=(
            bf16(pixels, channels),
            bf16(pixels, channels),
            jax.ShapeDtypeStruct((channels, hidden_units), grad_type),
            jax.ShapeDtypeStruct((hidden_units, channels), grad_type),
            f32(1, hidden_units),
            f32(1, channels),
            f32(1, channels),
        ),
        in_specs=[
            whole(pixels, channels),
            whole(pixels, channels),
            whole(pixels, channels),
            whole(1, channels),
            whole(1, channels),
            pl.BlockSpec((1, chunk), lambda s: (0, s)),
            pl.BlockSpec((channels, chunk), lambda s: (0, s)),
            pl.BlockSpec((chunk, channels), lambda s: (s, 0)),
        ],
        out_specs=(
            whole(pixels, channels),
            whole(pixels, channels),
            pl.BlockSpec((channels, chunk), lambda s: (0, s)),
            pl.BlockSpec((chunk, channels), lambda s: (s, 0)),
            pl.BlockSpec((1, chunk), lambda s: (0, s)),
            whole(1, channels),
            whole(1, channels),
        ),
        scratch_shapes=[
            pltpu.VMEM((pixels, channels), jnp.bfloat16),
            pltpu.VMEM((channels, pixels), jnp.bfloat16),
            pltpu.VMEM((pixels, channels), jnp.bfloat16),
            pltpu.VMEM((pixels, channels), jnp.float32),
            pltpu.VMEM((pixels, channels), jnp.float32),
            pltpu.VMEM((pixels, chunk), jnp.bfloat16),
            pltpu.VMEM((pixels, chunk), jnp.bfloat16),
        ],
        compiler_params=pltpu.CompilerParams(vmem_limit_bytes=VMEM_BYTES),
        cost_estimate=pl.CostEstimate(
            flops=12 * pixels * channels * hidden_units,
            bytes_accessed=12 * channels * hidden_units,
            transcendentals=2 * pixels * hidden_units,
        ),
    )(conv, image, cot, gain, layer, bias, w_in, w_out)


def local(image, dw_kernel, ln_gain, w_in, b_in, w_out, layer_scale, cotangent):
    tile_shape = image.shape
    tile_rows, tile_cols, channels = tile_shape
    group_count = lax.axis_size("row") * lax.axis_size("col")
    pixels = tile_rows * tile_cols
    scale_factor = 1.0 / math.sqrt(pixels * group_count)
    flat = lambda field: field.reshape(pixels, channels)
    full_in = lax.all_gather(w_in, "col", axis=0, tiled=True)
    full_out = lax.all_gather(w_out, "col", axis=0, tiled=True)
    taps = dw_kernel.T
    padded = halo_pad(image)
    conv = stencil_call(forward_kernel, padded, taps, (), tile_shape)
    out_map, grad_conv, grad_in, grad_out, bias_part, gain_part, scale_part = mlp_call(
        flat(conv),
        flat(image),
        flat(cotangent),
        ln_gain[None],
        layer_scale[None],
        b_in[None],
        full_in,
        full_out,
        jnp.float32,
    )
    part_in = lax.psum_scatter(grad_in, "col", scatter_dimension=0, tiled=True)
    part_out = lax.psum_scatter(grad_out, "col", scatter_dimension=0, tiled=True)
    grad_conv = grad_conv.reshape(tile_shape)
    grad_padded = halo_pad(grad_conv)
    tap_part = taps_call(padded, grad_conv)
    grad_image = stencil_call(backward_kernel, grad_padded, taps[::-1], (cotangent,), tile_shape)
    summed_in, summed_out = lax.psum((part_in, part_out), "row")
    scale_sum, bias_sum, gain_sum, tap_sum = lax.psum(
        (scale_part[0], bias_part[0], gain_part[0], tap_part), ("row", "col")
    )
    group_size = channels // group_count
    group_index = lax.axis_index("row") * lax.axis_size("col") + lax.axis_index("col")
    grad_kernel = lax.dynamic_slice_in_dim(tap_sum.T, group_index * group_size, group_size, 0)
    return (
        out_map.reshape(tile_shape),
        grad_image,
        grad_kernel * scale_factor,
        summed_in * scale_factor,
        summed_out * scale_factor,
        bias_sum * scale_factor,
        gain_sum * scale_factor,
        scale_sum * scale_factor,
    )


def solution(mesh):
    in_specs = (
        P("row", "col", None),
        P(),
        P(),
        P("col", None),
        P(),
        P("col", None),
        P(),
        P("row", "col", None),
    )
    out_specs = (
        P("row", "col", None),
        P("row", "col", None),
        P(("row", "col"), None),
        P("col", None),
        P("col", None),
        P(),
        P(),
        P(),
    )
    return jax.shard_map(local, mesh=mesh, in_specs=in_specs, out_specs=out_specs, check_vma=False)
```

time: 627 us -> 719 us (1.15)
  waiting for transfers between devices: 223 us -> 559 us
  other arithmetic: 152 us -> 12.5 us
  local copies, waits for them, and re-layouts: 75.7 us -> 6.28 us
  Pallas kernels: 0 us -> 67.7 us
  blocking collectives: 97.1 us -> 41.7 us
  matrix products: 41.3 us -> 0 us
    reduce_scatter x2, waiting for transfers between devices: 169 us -> 335 us  [the longest x1 177 us: local(): lax.psum_scatter(grad_out, 'col', scatter_dimension=0, tiled=True)]
    all_gather x2, waiting for transfers between devices: 17.8 us -> 130 us  [the longest x1 81.9 us: local(): full_out = lax.all_gather(w_out, 'col', axis=0, tiled=True)]
    convert_element_type x5 -> x0, other arithmetic: 97.8 us -> none  [the longest x1 47.3 us: local(): group_stencil(grouped, kernel_mine, height, breadth).astype(jnp.bfloat16)]
    psum x0 -> x1, waiting for transfers between devices: none -> 73.8 us  [local(): lax.psum((scale_part[0], bias_part[0], gain_part[0], tap_part), ('row', '...]
    pallas_call x0 -> x4, Pallas kernels: none -> 67.7 us  [the longest x1 34.3 us: mlp_call(): pl.pallas_call(mlp_kernel, grid=(hidden_units // chunk,), out_shape=(bf16...]
    reduce_sum x6 -> x0, other arithmetic: 49.3 us -> none  [the longest x4 46.2 us: group_taps(): columns.append(jnp.sum(gradient * window, axis=(1, 2)))]
    dot_general x6 -> x0, matrix products: 41.3 us -> none  [the longest x1 8.61 us: local(): preact = jnp.dot(normed, full_in, preferred_element_type=jnp.float32) + b_in]
    all_to_all x1 -> x0, blocking collectives: 38.7 us -> none  [from_groups(): lax.all_to_all(packed.reshape(row_count * col_count, group_size, pixels),...]
  transfers between devices with their start and end apart: 8 -> 14, of which waited for: 4 -> 8; matrix products, arithmetic and copies ran while one was open for 40% -> 2% of each run, Pallas kernels for 0% -> 5%
where the time goes in v1:
time: 719 us; the launch traced here: 718 us
  waiting for transfers between devices  559 us (78%)
  Pallas kernels  67.7 us (9%)
  blocking collectives  41.7 us (6%)
  starting transfers between devices  16.8 us (2%)
  between operations  14.3 us (2%)
  other arithmetic  12.5 us (2%)
    reduce_scatter x1, waiting for transfers between devices, local(): lax.psum_scatter(grad_out, 'col', scatter_dimension=0, tiled=True)  177 us
    reduce_scatter x1, waiting for transfers between devices, local(): part_in = lax.psum_scatter(grad_in, 'col', scatter_dimension=0, tiled=True)  159 us
    all_gather x1, waiting for transfers between devices, local(): full_out = lax.all_gather(w_out, 'col', axis=0, tiled=True)  81.9 us
    psum x1, waiting for transfers between devices, local(): lax.psum((scale_part[0], bias_part[0], gain_part[0], tap_part), ('row', '...  73.8 us
    all_gather x1, waiting for transfers between devices, local(): full_in = lax.all_gather(w_in, 'col', axis=0, tiled=True)  48 us
    psum x1, blocking collectives, local(): lax.psum((scale_part[0], bias_part[0], gain_part[0], tap_part), ('row', '...  41.7 us
    pallas_call x1, Pallas kernels, mlp_call(): pl.pallas_call(mlp_kernel, grid=(hidden_units // chunk,), out_shape=(bf16...  34.3 us
    pallas_call x2, Pallas kernels, stencil_call(): pl.pallas_call(kernel, grid=(channels // LANES,), out_shape=jax.ShapeDtyp...  22.8 us
  transfers between devices with their start and end apart: 14, of which 8 were waited for; matrix products, arithmetic and copies ran while one was open for 2% of the time, Pallas kernels for 5%

profile of v1, /device:TPU:0, one launch (start us, length us, event | category | flops | bytes accessed | tf_op | source)
XLA Modules:
  0.0 718.5 jit_solution(3858166952638823638)
XLA Ops:
  7.2 0.0 all-gather.3.cloned.1.call-start
  7.2 0.7 all-gather.3.cloned.1.call-update
  7.9 0.0 all-gather.5.cloned.1.call-start
  7.9 0.7 all-gather.5.cloned.1.call-update
  8.6 0.0 reduce-scatter.3.cloned.1.call-start
  8.7 1.1 fusion.1
  9.8 4.9 collective-permute-start
  14.6 1.3 collective-permute-start.1
  15.9 2.8 collective-permute-done
  18.8 6.3 collective-permute-done.1
  25.1 1.3 pad_maximum_fusion.7
  26.4 1.3 collective-permute-start.2
  27.7 1.3 collective-permute-start.3
  29.0 1.3 broadcast_in_dim.10.layer_ref
  30.3 1.3 broadcast_in_dim.9.gain_ref
  31.6 0.0 collective-permute-done.2
  31.6 0.0 collective-permute-done.3
  31.6 3.1 pad_maximum_fusion.padded_ref
  34.6 11.3 %shard_map.143 = bf16[16,32,768]{2,1,0:T(8,128)(2,1)} custom-call(bf16[28,44,768]{2,1,0:T(8,128)(2,1)} %pad_maximum_fusion.padded_ref, f32[49,768]{1,0:T(8,128)} %bitcast.17), custom_call_target="tpu_custom_call" | custom-call | flops 38535168 | bytes 3145728 | tf_op jit(solution)/shard_map/pallas_call | solution.py:123
  45.9 48.0 %all-gather.3.cloned.1.call-done.w_in_ref = bf16[768,3072]{1,0:T(8,128)(2,1)} async-done(((bf16[48,3072]{1,0:T(8,128)(2,1)}), bf16[768,3072]{1,0:T(8,128)(2,1)}) %all-gather.3.cloned.1.call-update) | async-done | bytes 4718608 | tf_op jit(solution)/shard_map/all_gather | solution.py:305
  93.9 81.9 %all-gather.5.cloned.1.call-done.w_out_ref = bf16[3072,768]{1,0:T(8,128)(2,1)} async-done(((bf16[192,768]{1,0:T(8,128)(2,1)}), bf16[3072,768]{1,0:T(8,128)(2,1)}) %all-gather.5.cloned.1.call-update) | async-done | bytes 4718608 | tf_op jit(solution)/shard_map/all_gather | solution.py:306
  175.8 34.3 %shard_map.144 = (bf16[512,768]{1,0:T(8,128)(2,1)}, bf16[512,768]{1,0:T(8,128)(2,1)}, f32[768,3072]{1,0:T(8,128)}, f32[3072,768]{1,0:T(8,128)}, f32[1,3072]{1,0:...) custom-call(bf16[512,768]{1,0:T(8,128)(2,1)} %bitcast.15, bf16[512,768]{1,0:T(8,128)(2,1)} %bitcast.14, ...), custom_call_target="tpu_custom_call" | custom-call | flops 14495514624 | bytes 28311552 | tf_op jit(solution)/shard_map/pallas_call | solution.py:249
  210.2 0.0 reduce-scatter.3.cloned.1.call-update
  210.2 0.0 reduce-scatter.5.cloned.1.call-start
  210.2 0.5 reduce-scatter.5.cloned.1.call-update
  210.8 0.0 copy-start
  210.8 0.0 copy-start.1
  210.8 0.0 copy-start.4
  210.8 0.0 copy-start.3
  210.8 0.0 copy-start.2
  210.8 0.0 all-reduce.5.cloned.1.call-start
  210.9 10.6 %shard_map.146 = f32[49,768]{1,0:T(8,128)} custom-call(bf16[28,44,768]{2,1,0:T(8,128)(2,1)} %pad_maximum_fusion.padded_ref, bf16[16,32,768]{2,1,0:T(8,128)(2,1)} %bitcast.10), custom_call_target="tpu_custom_call" | custom-call | flops 38535168 | bytes 3145728 | tf_op jit(solution)/shard_map/pallas_call | solution.py:147
  221.4 0.0 all-reduce.5.cloned.1.call-update
  221.5 0.0 all-reduce.7.cloned.1.call-start
  221.5 158.5 %reduce-scatter.3.cloned.1.call-done = f32[48,3072]{1,0:T(8,128)} async-done(((f32[768,3072]{1,0:T(8,128)}), f32[48,3072]{1,0:T(8,128)}) %reduce-scatter.3.cloned.1.call-update) | async-done | bytes 589840 | tf_op jit(solution)/shard_map/reduce_scatter | solution.py:321
  380.0 176.7 %reduce-scatter.5.cloned.1.call-done = f32[192,768]{1,0:T(8,128)} async-done(((f32[3072,768]{1,0:T(8,128)}), f32[192,768]{1,0:T(8,128)}) %reduce-scatter.5.cloned.1.call-update) | async-done | bytes 589840 | tf_op jit(solution)/shard_map/reduce_scatter | solution.py:322
  556.7 0.0 all-reduce.7.cloned.1.call-update
  556.7 0.0 copy-done
  556.8 0.1 fusion
  556.8 3.4 collective-permute-start.4
  560.2 1.3 collective-permute-start.5
  561.5 0.0 copy-done.1
  561.5 1.9 rev.3.taps_ref
  563.4 0.0 copy-done.4
  563.4 0.0 copy-done.3
  563.5 0.0 copy-done.2
  563.5 41.7 %all-reduce = (f32[3072]{0:T(1024)S(1)}, f32[768]{0:T(1024)S(1)}, f32[768]{0:T(1024)S(1)}) all-reduce(f32[3072]{0:T(1024)S(1)} %bitcast.19, f32[768]{0:T(1024)S(1)} %reduce, f32[768]{0:T(1024)S(1)} %reduce.1), channel_id=1, replica_groups=mesh['row'=2,'col'=16] {'row','col'}, use_global_device_ids=true, to_apply=%region_5.0 | all-reduce | flops 4608 | bytes 36864 | tf_op jit(solution)/shard_map/psum | solution.py:328
  605.2 0.0 collective-permute-done.4
  605.2 0.0 collective-permute-done.5
  605.2 0.3 pad_maximum_fusion.4
  605.5 1.8 collective-permute-start.6
  607.4 1.3 collective-permute-start.7
  608.7 0.6 broadcast_multiply_fusion.3
  609.3 0.6 broadcast_multiply_fusion.2
  609.9 73.8 %all-reduce.5.cloned.1.call-done = f32[49,768]{1,0:T(8,128)} async-done(((f32[49,768]{1,0:T(8,128)}), f32[49,768]{1,0:T(8,128)}) %all-reduce.5.cloned.1.call-update) | async-done | bytes 150544 | tf_op jit(solution)/shard_map/psum | solution.py:328
  683.7 0.9 multiply_bitcast_fusion
  684.5 0.7 copy.16
  685.2 0.0 collective-permute-done.6
  685.2 0.0 collective-permute-done.7
  685.2 1.9 pad_maximum_fusion.1.padded_ref
  687.1 11.5 %shard_map.145 = bf16[16,32,768]{2,1,0:T(8,128)(2,1)} custom-call(bf16[28,44,768]{2,1,0:T(8,128)(2,1)} %pad_maximum_fusion.1.padded_ref, f32[49,768]{1,0:T(8,128)} %rev.3.taps_ref, bf16[16,32,768]{2,1,0:T(8,128)(2,1)} %cot_ref.1), custom_call_target="tpu_custom_call" | custom-call | flops 38535168 | bytes 3145728 | tf_op jit(solution)/shard_map/pallas_call | solution.py:123
  698.6 9.2 %all-reduce.7.cloned.1.call-done = (f32[48,3072]{1,0:T(8,128)}, f32[192,768]{1,0:T(8,128)}) async-done(((f32[48,3072]{1,0:T(8,128)}, f32[192,768]{1,0:T(8,128)}), (f32[48,3072]{1,0:T(8,128)}, f32[192,768]{1,0:T(8,128)})) %all-reduce.7.cloned.1.call-update) | async-done | bytes 1179664 | tf_op jit(solution)/shard_map/psum | solution.py:327
  707.8 1.9 broadcast_multiply_fusion
  709.7 1.9 broadcast_multiply_fusion.1
  (2 shorter events, 0.0 us)
Async XLA Ops:
  7.2 86.7 %all-gather.3.cloned.1.call-start = ((), (), s32[]{:S(2)}) async-start(), calls=%async_computation.2 | async-start | bytes 5013504 | tf_op jit(solution)/shard_map/all_gather | solution.py:305
  7.9 167.9 %all-gather.5.cloned.1.call-start = ((), (), s32[]{:S(2)}) async-start(), calls=%async_computation.3 | async-start | bytes 5013504 | tf_op jit(solution)/shard_map/all_gather | solution.py:306
  8.6 371.4 %reduce-scatter.3.cloned.1.call-start = ((), (), s32[]{:S(2)}) async-start(), calls=%async_computation.5 | async-start | bytes 10027008 | tf_op jit(solution)/shard_map/reduce_scatter | solution.py:321
  9.8 9.0 %collective-permute-start = (bf16[16,6,768]{2,1,0:T(8,128)(2,1)S(1)}, bf16[16,6,768]{2,1,0:T(8,128)(2,1)S(1)}, u32[]{:S(2)}, u32[]{:S(2)}) collective-permute-start(bf16[16,6,768]{2,1,0:T(8,128)(2,1)S(1)} %get-tuple-element.41), channel_id=1, source_target_pairs={{0,1},{1,2},{2,3},{3,4},{4,5},{5,6},{6,7},{7,8},{8,9},{9,10},{10,1... | collective-permute-start | bytes 442376 | tf_op jit(solution)/shard_map/ppermute | solution.py:32
  14.6 10.4 %collective-permute-start.1 = (bf16[16,6,768]{2,1,0:T(8,128)(2,1)S(1)}, bf16[16,6,768]{2,1,0:T(8,128)(2,1)S(1)}, u32[]{:S(2)}, u32[]{:S(2)}) collective-permute-start(bf16[16,6,768]{2,1,0:T(8,128)(2,1)S(1)} %get-tuple-element.42), channel_id=1, source_target_pairs={{1,0},{2,1},{3,2},{4,3},{5,4},{6,5},{7,6},{8,7},{9,8},{10,9},{11,1... | collective-permute-start | bytes 442376 | tf_op jit(solution)/shard_map/ppermute | solution.py:33
  26.4 5.2 collective-permute-start.2
  27.7 3.8 collective-permute-start.3
  210.2 346.5 %reduce-scatter.5.cloned.1.call-start = ((), (), s32[]{:S(2)}) async-start(), calls=%async_computation.6 | async-start | bytes 10027008 | tf_op jit(solution)/shard_map/reduce_scatter | solution.py:322
  210.8 346.0 %copy-start = (bf16[512,768]{1,0:T(8,128)(2,1)S(1)}, bf16[512,768]{1,0:T(8,128)(2,1)}, u32[]{:S(2)}) copy-start(bf16[512,768]{1,0:T(8,128)(2,1)} %get-tuple-element.16) | copy-start | bytes 2359300
  210.8 350.7 %copy-start.1 = (f32[768,49]{0,1:T(8,128)S(1)}, f32[768,49]{0,1:T(8,128)}, u32[]{:S(2)}) copy-start(f32[768,49]{0,1:T(8,128)} %param.9) | copy-start | bytes 451588
  210.8 352.6 %copy-start.4 = (f32[1,768]{1,0:T(1,128)S(1)}, f32[1,768]{1,0:T(1,128)}, u32[]{:S(2)}) copy-start(f32[1,768]{1,0:T(1,128)} %get-tuple-element.20) | copy-start | bytes 9220
  210.8 352.6 %copy-start.3 = (f32[1,768]{1,0:T(1,128)S(1)}, f32[1,768]{1,0:T(1,128)}, u32[]{:S(2)}) copy-start(f32[1,768]{1,0:T(1,128)} %get-tuple-element.21) | copy-start | bytes 9220
  210.8 352.7 %copy-start.2 = (f32[1,3072]{1,0:T(1,128)S(1)}, f32[1,3072]{1,0:T(1,128)}, u32[]{:S(2)}) copy-start(f32[1,3072]{1,0:T(1,128)} %get-tuple-element.19) | copy-start | bytes 36868
  210.8 472.8 %all-reduce.5.cloned.1.call-start = ((), (), s32[]{:S(2)}) async-start(), calls=%async_computation.4 | async-start | bytes 344064 | tf_op jit(solution)/shard_map/psum | solution.py:328
  221.5 486.3 %all-reduce.7.cloned.1.call-start = ((), (), s32[]{:S(2)}) async-start(), calls=%async_computation.7 | async-start | bytes 2359296 | tf_op jit(solution)/shard_map/psum | solution.py:327
  556.8 48.4 %collective-permute-start.4 = (bf16[16,6,768]{2,1,0:T(8,128)(2,1)S(1)}, bf16[16,6,768]{2,1,0:T(8,128)(2,1)S(1)}, u32[]{:S(2)}, u32[]{:S(2)}) collective-permute-start(bf16[16,6,768]{2,1,0:T(8,128)(2,1)S(1)} %get-tuple-element.39), channel_id=1, source_target_pairs={{0,1},{1,2},{2,3},{3,4},{4,5},{5,6},{6,7},{7,8},{8,9},{9,10},{10,1... | collective-permute-start | bytes 442376 | tf_op jit(solution)/shard_map/ppermute | solution.py:32
  560.2 45.0 %collective-permute-start.5 = (bf16[16,6,768]{2,1,0:T(8,128)(2,1)S(1)}, bf16[16,6,768]{2,1,0:T(8,128)(2,1)S(1)}, u32[]{:S(2)}, u32[]{:S(2)}) collective-permute-start(bf16[16,6,768]{2,1,0:T(8,128)(2,1)S(1)} %get-tuple-element.40), channel_id=1, source_target_pairs={{1,0},{2,1},{3,2},{4,3},{5,4},{6,5},{7,6},{8,7},{9,8},{10,9},{11,1... | collective-permute-start | bytes 442376 | tf_op jit(solution)/shard_map/ppermute | solution.py:33
  605.5 79.7 %collective-permute-start.6 = (bf16[6,44,768]{2,1,0:T(8,128)(2,1)S(1)}, bf16[6,44,768]{2,1,0:T(8,128)(2,1)S(1)}, u32[]{:S(2)}, u32[]{:S(2)}) collective-permute-start(bf16[6,44,768]{2,1,0:T(8,128)(2,1)S(1)} %get-tuple-element.35), channel_id=1, source_target_pairs={{0,16},{1,17},{2,18},{3,19},{4,20},{5,21},{6,22},{7,23},{8,24},{9,... | collective-permute-start | bytes 1216520 | tf_op jit(solution)/shard_map/ppermute | solution.py:35
  607.4 77.9 %collective-permute-start.7 = (bf16[6,44,768]{2,1,0:T(8,128)(2,1)S(1)}, bf16[6,44,768]{2,1,0:T(8,128)(2,1)S(1)}, u32[]{:S(2)}, u32[]{:S(2)}) collective-permute-start(bf16[6,44,768]{2,1,0:T(8,128)(2,1)S(1)} %get-tuple-element.36), channel_id=1, source_target_pairs={{16,0},{17,1},{18,2},{19,3},{20,4},{21,5},{22,6},{23,7},{24,8},{25... | collective-permute-start | bytes 1216520 | tf_op jit(solution)/shard_map/ppermute | solution.py:36
Sparse Core Ops, SparseCore 0:
  10.8 83.0 all-gather.2
  96.7 79.0 all-gather.4
  210.3 169.6 reduce-scatter.2
  386.5 170.1 reduce-scatter.4
  562.7 120.9 all-reduce.4
  685.9 21.8 all-reduce.6

commit v2 on v1

--- a/solution.py
+++ b/solution.py
@@ -242,7 +242,11 @@
 
 def mlp_call(conv, image, cot, gain, layer, bias, w_in, w_out, grad_type, chunk=256):
     pixels, channels = conv.shape
-    hidden_units = w_in.shape[1]
+    hidden_units = w_out.shape[0]
+    quarter_steps = hidden_units // (4 * chunk)
+    quartered = pl.BlockSpec(
+        (None, channels, chunk), lambda s: (s // quarter_steps, 0, s % quarter_steps)
+    )
     whole = lambda h, w: pl.BlockSpec((h, w), lambda s: (0, 0))
     f32 = lambda *shape: jax.ShapeDtypeStruct(shape, jnp.float32)
     bf16 = lambda *shape: jax.ShapeDtypeStruct(shape, jnp.bfloat16)
@@ -252,7 +256,7 @@
         out_shape=(
             bf16(pixels, channels),
             bf16(pixels, channels),
-            jax.ShapeDtypeStruct((channels, hidden_units), grad_type),
+            jax.ShapeDtypeStruct((4, channels, hidden_units // 4), grad_type),
             jax.ShapeDtypeStruct((hidden_units, channels), grad_type),
             f32(1, hidden_units),
             f32(1, channels),
@@ -265,13 +269,13 @@
             whole(1, channels),
             whole(1, channels),
             pl.BlockSpec((1, chunk), lambda s: (0, s)),
-            pl.BlockSpec((channels, chunk), lambda s: (0, s)),
+            quartered,
             pl.BlockSpec((chunk, channels), lambda s: (s, 0)),
         ],
         out_specs=(
             whole(pixels, channels),
             whole(pixels, channels),
-            pl.BlockSpec((channels, chunk), lambda s: (0, s)),
+            quartered,
             pl.BlockSpec((chunk, channels), lambda s: (s, 0)),
             pl.BlockSpec((1, chunk), lambda s: (0, s)),
             whole(1, channels),
@@ -295,6 +299,308 @@
     )(conv, image, cot, gain, layer, bias, w_in, w_out)
 
 
+MESH = pl.DeviceIdType.MESH
+PARTS = 2
+
+
+class Place:
+    def __init__(self):
+        self.row = lax.axis_index("row")
+        self.col = lax.axis_index("col")
+        self.depth = lax.axis_size("col") // 4
+        self.z = self.col // 4
+        self.y = (self.col // 2) % 2
+        self.x = self.col % 2
+        self.core = self.row % 2
+
+    def at(self, z, y, x):
+        return (self.row, 4 * z + 2 * y + x)
+
+    def z_peer(self, hop):
+        return self.at((self.z + hop) % self.depth, self.y, self.x)
+
+    def y_peer(self):
+        return self.at(self.z, 1 - self.y, self.x)
+
+    def x_peer(self):
+        return self.at(self.z, self.y, 1 - self.x)
+
+    def core_peer(self):
+        return (self.row + 1 - 2 * self.core, self.col)
+
+    def greet(self):
+        barrier = pltpu.get_barrier_semaphore()
+        peers = [self.z_peer(hop) for hop in range(1, self.depth)]
+        peers += [self.y_peer(), self.x_peer(), self.core_peer()]
+        for peer in peers:
+            pl.semaphore_signal(barrier, inc=1, device_id=peer, device_id_type=MESH)
+        pl.semaphore_wait(barrier, len(peers))
+
+
+class Mail:
+    def __init__(self, send_sems, recv_sems):
+        self.send_sems, self.recv_sems, self.copies = send_sems, recv_sems, []
+
+    def send(self, source, target, peer):
+        slot = len(self.copies)
+        copy = pltpu.make_async_remote_copy(
+            src_ref=source,
+            dst_ref=target,
+            send_sem=self.send_sems.at[slot],
+            recv_sem=self.recv_sems.at[slot],
+            device_id=peer,
+            device_id_type=MESH,
+        )
+        copy.start()
+        self.copies.append(copy)
+        return copy
+
+    def finish(self):
+        for copy in self.copies:
+            copy.wait_send()
+
+
+def gather_kernel(shard_in, shard_out, full_in, full_out, send_sems, recv_sems, own_sems):
+    place = Place()
+    z, y, x = place.z, place.y, place.x
+    mine = pl.ds(2 * place.core, 2)
+    own_in = pltpu.make_async_copy(shard_in.at[mine], full_in.at[mine, z, y, x], own_sems.at[0])
+    own_out = pltpu.make_async_copy(
+        shard_out.at[mine], full_out.at[z, y, x, mine], own_sems.at[1]
+    )
+    own_in.start()
+    own_out.start()
+    place.greet()
+    own_in.wait()
+    own_out.wait()
+    mail = Mail(send_sems, recv_sems)
+    every = slice(None)
+
+    def view(array, quarter, zs, ys, xs):
+        if array == 0:
+            return full_in.at[quarter, zs, ys, xs]
+        return full_out.at[zs, ys, xs, quarter]
+
+    def send(piece, stage):
+        array, part = piece
+        quarter = 2 * place.core + part
+        first_y = part == 0
+        if stage == 0:
+            block = view(array, quarter, z, y, x)
+            return [mail.send(block, block, place.z_peer(hop)) for hop in range(1, place.depth)]
+        if stage == 1:
+            block = view(array, quarter, every, y, x)
+            return [mail.send(block, block, place.y_peer() if first_y else place.x_peer())]
+        if stage == 2:
+            block = view(array, quarter, every, *((every, x) if first_y else (y, every)))
+            return [mail.send(block, block, place.x_peer() if first_y else place.y_peer())]
+        block = view(array, quarter, every, every, every)
+        return [mail.send(block, block, place.core_peer())]
+
+    pieces = [(array, part) for array in range(2) for part in range(PARTS)]
+    flying = [[] for _ in pieces]
+    for tick in range(len(pieces) + 4):
+        for index in range(len(pieces) - 1, -1, -1):
+            stage = tick - index
+            if 0 <= stage <= 4:
+                for copy in flying[index]:
+                    copy.wait_recv()
+                if stage < 4:
+                    flying[index] = send(pieces[index], stage)
+    mail.finish()
+
+
+def gather_call(w_in, w_out):
+    depth = lax.axis_size("col") // 4
+    in_rows, hidden_units = w_in.shape
+    out_rows, channels = w_out.shape
+    width, height = hidden_units // 4, out_rows // 4
+    shard_in = w_in.reshape(in_rows, 4, width).transpose(1, 0, 2)
+    shard_out = w_out.reshape(4, height, channels)
+    copies = 4 * (depth - 1 + 3)
+    anywhere = pl.BlockSpec(memory_space=pl.ANY)
+    full_in, full_out = pl.pallas_call(
+        gather_kernel,
+        out_shape=(
+            jax.ShapeDtypeStruct((4, depth, 2, 2, in_rows, width), w_in.dtype),
+            jax.ShapeDtypeStruct((depth, 2, 2, 4, height, channels), w_out.dtype),
+        ),
+        in_specs=[anywhere, anywhere],
+        out_specs=(anywhere, anywhere),
+        scratch_shapes=[
+            pltpu.SemaphoreType.DMA((copies,)),
+            pltpu.SemaphoreType.DMA((copies,)),
+            pltpu.SemaphoreType.DMA((2,)),
+        ],
+        compiler_params=pltpu.CompilerParams(
+            collective_id=0, has_side_effects=True, vmem_limit_bytes=VMEM_BYTES
+        ),
+    )(shard_in, shard_out)
+    return full_in.reshape(4, 4 * depth * in_rows, width), full_out.reshape(-1, channels)
+
+
+def scatter_kernel(
+    grad_in, grad_out, small, total, small_total,
+    recv_core, sum_core, recv_one, sum_one, recv_two, sum_two, recv_z, small_pair, small_z,
+    send_sems, recv_sems,
+):
+    place = Place()
+    z, y, x = place.z, place.y, place.x
+    depth = place.depth
+    place.greet()
+    mail = Mail(send_sems, recv_sems)
+    f32 = jnp.float32
+    every = slice(None)
+
+    def block_of(array, quarter, zz, yy, xx):
+        if array == 0:
+            return grad_in.at[quarter, zz, yy, xx]
+        return grad_out.at[zz, yy, xx, quarter]
+
+    pieces = [(array, part) for array in range(2) for part in range(PARTS)]
+    small_copy = mail.send(small, small_pair.at[0], place.core_peer())
+    flying = []
+    for index, (array, part) in enumerate(pieces):
+        source = block_of(array, 2 * (1 - place.core) + part, every, every, every)
+        flying.append([mail.send(source, recv_core.at[index], place.core_peer())])
+
+    def add(target, left, right):
+        target[...] = (left[...].astype(f32) + right[...].astype(f32)).astype(target.dtype)
+
+    def advance(index, stage):
+        array, part = pieces[index]
+        quarter = 2 * place.core + part
+        x_first = part == 0
+        near, far = (x, y) if x_first else (y, x)
+        near_peer, far_peer = place.x_peer(), place.y_peer()
+        if not x_first:
+            near_peer, far_peer = far_peer, near_peer
+        for copy in flying[index]:
+            copy.wait_recv()
+        if stage == 0:
+
+            def add_core(zz, carry):
+                for yy in range(2):
+                    for xx in range(2):
+                        first, second = (xx, yy) if x_first else (yy, xx)
+                        add(
+                            sum_core.at[index, first, zz, second],
+                            block_of(array, quarter, zz, yy, xx),
+                            recv_core.at[index, zz, yy, xx],
+                        )
+                return carry
+
+            lax.fori_loop(0, depth, add_core, 0)
+            return [mail.send(sum_core.at[index, 1 - near], recv_one.at[index], near_peer)]
+        if stage == 1:
+
+            def add_one(zz, carry):
+                for second in range(2):
+                    add(
+                        sum_one.at[index, second, zz],
+                        sum_core.at[index, near, zz, second],
+                        recv_one.at[index, zz, second],
+                    )
+                return carry
+
+            lax.fori_loop(0, depth, add_one, 0)
+            return [mail.send(sum_one.at[index, 1 - far], recv_two.at[index], far_peer)]
+        if stage == 2:
+
+            def add_two(zz, carry):
+                add(
+                    sum_two.at[index, zz],
+                    sum_one.at[index, far, zz],
+                    recv_two.at[index, zz],
+                )
+                return carry
+
+            lax.fori_loop(0, depth, add_two, 0)
+            return [
+                mail.send(
+                    sum_two.at[index, (z + hop) % depth],
+                    recv_z.at[index, hop - 1],
+                    place.z_peer(hop),
+                )
+                for hop in range(1, depth)
+            ]
+        if stage == 3:
+            owned = sum_two[index, z].astype(f32)
+            for hop in range(1, depth):
+                owned = owned + recv_z[index, hop - 1].astype(f32)
+            total[array, quarter] = owned
+            block = total.at[array, quarter]
+            return [mail.send(block, block, place.core_peer())]
+        return []
+
+    def advance_small(stage):
+        if stage < 3:
+            small_flying[0].wait_recv()
+            source = small if stage == 0 else small_pair.at[2 + stage]
+            if stage < 2:
+                add(small_pair.at[3 + stage], source, small_pair.at[stage])
+                peer = place.x_peer() if stage == 0 else place.y_peer()
+                return [mail.send(small_pair.at[3 + stage], small_pair.at[1 + stage], peer)]
+            add(small_z.at[0], source, small_pair.at[stage])
+            return [
+                mail.send(small_z.at[0], small_z.at[hop], place.z_peer(hop))
+                for hop in range(1, depth)
+            ]
+        for copy in small_flying:
+            copy.wait_recv()
+        summed = small_z[z]
+        for other in range(1, depth):
+            summed = summed + small_z[(z + depth - other) % depth]
+        small_total[...] = summed
+        return []
+
+    small_flying = [small_copy]
+    for tick in range(len(pieces) + 4):
+        for index in range(len(pieces) - 1, -1, -1):
+            if 0 <= tick - index <= 4:
+                flying[index] = advance(index, tick - index)
+        if tick < 4:
+            small_flying = advance_small(tick)
+    mail.finish()
+
+
+def scatter_call(grad_in, grad_out, small):
+    depth = lax.axis_size("col") // 4
+    _, channels, width = grad_in.shape
+    height = channels // (4 * depth)
+    grad_in = grad_in.reshape(4, depth, 2, 2, height, width)
+    grad_out = grad_out.reshape(depth, 2, 2, 4, -1, channels)
+    assert grad_out.shape[4:] == (height, width)
+    kind = grad_in.dtype
+    vmem = pl.BlockSpec(memory_space=pltpu.VMEM)
+    copies = 4 * (1 + 1 + 1 + depth - 1 + 1) + 3 + depth - 1
+    return pl.pallas_call(
+        scatter_kernel,
+        out_shape=(
+            jax.ShapeDtypeStruct((2, 4, height, width), jnp.float32),
+            jax.ShapeDtypeStruct(small.shape, jnp.float32),
+        ),
+        in_specs=[vmem] * 3,
+        out_specs=(vmem, vmem),
+        scratch_shapes=[
+            pltpu.VMEM((4, depth, 2, 2, height, width), kind),
+            pltpu.VMEM((4, 2, depth, 2, height, width), kind),
+            pltpu.VMEM((4, depth, 2, height, width), kind),
+            pltpu.VMEM((4, 2, depth, height, width), kind),
+            pltpu.VMEM((4, depth, height, width), kind),
+            pltpu.VMEM((4, depth, height, width), kind),
+            pltpu.VMEM((4, depth - 1, height, width), kind),
+            pltpu.VMEM((5,) + small.shape, jnp.float32),
+            pltpu.VMEM((depth,) + small.shape, jnp.float32),
+            pltpu.SemaphoreType.DMA((copies,)),
+            pltpu.SemaphoreType.DMA((copies,)),
+        ],
+        compiler_params=pltpu.CompilerParams(
+            collective_id=1, has_side_effects=True, vmem_limit_bytes=VMEM_BYTES
+        ),
+    )(grad_in, grad_out, small)
+
+
 def local(image, dw_kernel, ln_gain, w_in, b_in, w_out, layer_scale, cotangent):
     tile_shape = image.shape
     tile_rows, tile_cols, channels = tile_shape
@@ -302,8 +608,7 @@
     pixels = tile_rows * tile_cols
     scale_factor = 1.0 / math.sqrt(pixels * group_count)
     flat = lambda field: field.reshape(pixels, channels)
-    full_in = lax.all_gather(w_in, "col", axis=0, tiled=True)
-    full_out = lax.all_gather(w_out, "col", axis=0, tiled=True)
+    full_in, full_out = gather_call(w_in, w_out)
     taps = dw_kernel.T
     padded = halo_pad(image)
     conv = stencil_call(forward_kernel, padded, taps, (), tile_shape)
@@ -316,18 +621,24 @@
         b_in[None],
         full_in,
         full_out,
-        jnp.float32,
+        jnp.bfloat16,
     )
-    part_in = lax.psum_scatter(grad_in, "col", scatter_dimension=0, tiled=True)
-    part_out = lax.psum_scatter(grad_out, "col", scatter_dimension=0, tiled=True)
     grad_conv = grad_conv.reshape(tile_shape)
     grad_padded = halo_pad(grad_conv)
     tap_part = taps_call(padded, grad_conv)
     grad_image = stencil_call(backward_kernel, grad_padded, taps[::-1], (cotangent,), tile_shape)
-    summed_in, summed_out = lax.psum((part_in, part_out), "row")
-    scale_sum, bias_sum, gain_sum, tap_sum = lax.psum(
-        (scale_part[0], bias_part[0], gain_part[0], tap_part), ("row", "col")
-    )
+    small_rows = [tap_part, bias_part.reshape(-1, channels), gain_part, scale_part]
+    small = jnp.concatenate(small_rows, axis=0)
+    small = jnp.pad(small, ((0, -small.shape[0] % 8), (0, 0)))
+    total, small_total = scatter_call(grad_in, grad_out, small)
+    if lax.axis_size("row") > 2:
+        total, small_total = (0.5 * field for field in lax.psum((total, small_total), "row"))
+    summed_in = total[0].transpose(1, 0, 2).reshape(w_in.shape)
+    summed_out = total[1].reshape(w_out.shape)
+    tap_sum = small_total[:TAPS]
+    rows_used = TAPS + bias_part.size // channels
+    bias_sum = small_total[TAPS:rows_used].reshape(-1)
+    gain_sum, scale_sum = small_total[rows_used], small_total[rows_used + 1]
     group_size = channels // group_count
     group_index = lax.axis_index("row") * lax.axis_size("col") + lax.axis_index("col")
     grad_kernel = lax.dynamic_slice_in_dim(tap_sum.T, group_index * group_size, group_size, 0)

time: 719 us -> 279 us (0.39)
  waiting for transfers between devices: 559 us -> 9.01 us
  Pallas kernels: 67.7 us -> 223 us
  blocking collectives: 41.7 us -> 0 us
  between operations: 14.3 us -> 0.79 us
    reduce_scatter x2 -> x0, waiting for transfers between devices: 335 us -> none  [the longest x1 177 us: local(): lax.psum_scatter(grad_out, 'col', scatter_dimension=0, tiled=True)]
    pallas_call x0 -> x2, Pallas kernels: none -> 155 us  [the longest x1 80.4 us: scatter_call(): pl.pallas_call(scatter_kernel, out_shape=(jax.ShapeDtypeStruct((2, 4, hei...]
    all_gather x2 -> x0, waiting for transfers between devices: 130 us -> none  [the longest x1 81.9 us: local(): full_out = lax.all_gather(w_out, 'col', axis=0, tiled=True)]
    psum x2 -> x0, waiting for transfers between devices: 83 us -> none  [the longest x1 73.8 us: local(): lax.psum((scale_part[0], bias_part[0], gain_part[0], tap_part), ('row', '...]
    psum x1 -> x0, blocking collectives: 41.7 us -> none  [local(): lax.psum((scale_part[0], bias_part[0], gain_part[0], tap_part), ('row', '...]
  transfers between devices with their start and end apart: 14 -> 8, of which waited for: 8 -> 2; matrix products, arithmetic and copies ran while one was open for 2% -> 6% of each run, Pallas kernels for 5% -> 56%
where the time goes in v2:
time: 279 us; the launch traced here: 276 us
  Pallas kernels  223 us (80%)
  starting transfers between devices  17 us (6%)
  other arithmetic  13.6 us (5%)
  local copies, waits for them, and re-layouts  12.6 us (5%)
  waiting for transfers between devices  9.01 us (3%)
    pallas_call x1, Pallas kernels, scatter_call(): pl.pallas_call(scatter_kernel, out_shape=(jax.ShapeDtypeStruct((2, 4, hei...  80.4 us
    pallas_call x1, Pallas kernels, gather_call(): pl.pallas_call(gather_kernel, out_shape=(jax.ShapeDtypeStruct((4, depth,...  75 us
    pallas_call x1, Pallas kernels, mlp_call(): pl.pallas_call(mlp_kernel, grid=(hidden_units // chunk,), out_shape=(bf16...  34.6 us
    pallas_call x2, Pallas kernels, stencil_call(): pl.pallas_call(kernel, grid=(channels // LANES,), out_shape=jax.ShapeDtyp...  22.8 us
    pallas_call x1, Pallas kernels, taps_call(): pl.pallas_call(taps_kernel, grid=(channels // LANES,), out_shape=jax.Shap...  10.5 us
    ppermute x2, starting transfers between devices, halo_pad(): left = lax.ppermute(tile[:, -REACH:], 'col', ahead(cols))  8.21 us
    ppermute x2, waiting for transfers between devices, halo_pad(): right = lax.ppermute(tile[:, :REACH], 'col', back(cols))  6.16 us
  transfers between devices with their start and end apart: 8, of which 2 were waited for; matrix products, arithmetic and copies ran while one was open for 6% of the time, Pallas kernels for 56%

profile of v2, /device:TPU:0, one launch (start us, length us, event | category | flops | bytes accessed | tf_op | source)
XLA Modules:
  0.0 276.2 jit_solution(8243410695775045345)
XLA Ops:
  0.6 0.0 copy-start.1
  0.6 1.1 fusion.1
  1.8 4.9 %collective-permute-start = (bf16[16,6,768]{2,1,0:T(8,128)(2,1)S(1)}, bf16[16,6,768]{2,1,0:T(8,128)(2,1)S(1)}, u32[]{:S(2)}, u32[]{:S(2)}) collective-permute-start(bf16[16,6,768]{2,1,0:T(8,128)(2,1)S(1)} %get-tuple-element.56), channel_id=1, source_target_pairs={{0,1},{1,2},{2,3},{3,4},{4,5},{5,6},{6,7},{7,8},{8,9},{9,10},{10,1... | collective-permute-start | bytes 442376 | tf_op jit(solution)/shard_map/ppermute | solution.py:32
  6.7 1.3 collective-permute-start.1
  8.0 2.8 %collective-permute-done = bf16[16,6,768]{2,1,0:T(8,128)(2,1)S(1)} collective-permute-done((bf16[16,6,768]{2,1,0:T(8,128)(2,1)S(1)}, bf16[16,6,768]{2,1,0:T(8,128)(2,1)S(1)}, u32[]{:S(2)}, u32[]{:S(2)}) %collective-permute-start) | collective-permute-done | bytes 147488 | tf_op jit(solution)/shard_map/ppermute | solution.py:32
  10.8 6.2 %collective-permute-done.1 = bf16[16,6,768]{2,1,0:T(8,128)(2,1)S(1)} collective-permute-done((bf16[16,6,768]{2,1,0:T(8,128)(2,1)S(1)}, bf16[16,6,768]{2,1,0:T(8,128)(2,1)S(1)}, u32[]{:S(2)}, u32[]{:S(2)}) %collective-permute-start.1) | collective-permute-done | bytes 147488 | tf_op jit(solution)/shard_map/ppermute | solution.py:33
  16.9 1.3 pad_maximum_fusion.7
  18.3 1.3 collective-permute-start.2
  19.6 1.3 collective-permute-start.3
  20.9 1.7 copy.23
  22.6 1.3 broadcast_in_dim.10.layer_ref
  23.9 1.3 broadcast_in_dim.9.gain_ref
  25.1 3.5 %rev.3.taps_ref = f32[49,768]{1,0:T(8,128)} reverse(f32[49,768]{1,0:T(8,128)} %bitcast.39), dimensions={0} | reverse | bytes 301056 | tf_op jit(solution)/shard_map/rev | solution.py:629
  28.7 75.0 %shard_map.144 = (bf16[4,4,2,2,48,768]{5,4,3,2,1,0:T(8,128)(2,1)}, bf16[4,2,2,4,48,768]{5,4,3,2,1,0:T(8,128)(2,1)}) custom-call(bf16[4,48,768]{2,1,0:T(8,128)(2,1)} %bitcast.36, bf16[4,48,768]{2,1,0:T(8,128)(2,1)} %bitcast.44), custom_call_target="tpu_custom_call" | custom-call | tf_op jit(solution)/shard_map/pallas_call | solution.py:422
  103.6 0.0 collective-permute-done.2
  103.6 0.0 collective-permute-done.3
  103.6 0.0 copy-done.1
  103.6 1.8 pad_maximum_fusion.padded_ref
  105.5 11.3 %shard_map.143 = bf16[16,32,768]{2,1,0:T(8,128)(2,1)} custom-call(bf16[28,44,768]{2,1,0:T(8,128)(2,1)} %pad_maximum_fusion.padded_ref, f32[49,768]{1,0:T(8,128)} %bitcast.40), custom_call_target="tpu_custom_call" | custom-call | flops 38535168 | bytes 3145728 | tf_op jit(solution)/shard_map/pallas_call | solution.py:123
  116.7 34.6 %shard_map.145 = (bf16[512,768]{1,0:T(8,128)(2,1)}, bf16[512,768]{1,0:T(8,128)(2,1)}, bf16[4,768,768]{2,1,0:T(8,128)(2,1)}, bf16[3072,768]{1,0:T(8,128)(2,1)}, f...) custom-call(bf16[512,768]{1,0:T(8,128)(2,1)} %bitcast.37, bf16[512,768]{1,0:T(8,128)(2,1)} %bitcast.33, ...), custom_call_target="tpu_custom_call" | custom-call | flops 14495514624 | bytes 28311552 | tf_op jit(solution)/shard_map/pallas_call | solution.py:253
  151.3 10.5 %shard_map.147 = f32[49,768]{1,0:T(8,128)} custom-call(bf16[28,44,768]{2,1,0:T(8,128)(2,1)} %pad_maximum_fusion.padded_ref, bf16[16,32,768]{2,1,0:T(8,128)(2,1)} %bitcast.29), custom_call_target="tpu_custom_call" | custom-call | flops 38535168 | bytes 3145728 | tf_op jit(solution)/shard_map/pallas_call | solution.py:147
  161.8 1.1 fusion
  162.9 0.5 broadcast.38
  163.4 1.4 reduce.7
  164.8 3.4 %collective-permute-start.4 = (bf16[16,6,768]{2,1,0:T(8,128)(2,1)S(1)}, bf16[16,6,768]{2,1,0:T(8,128)(2,1)S(1)}, u32[]{:S(2)}, u32[]{:S(2)}) collective-permute-start(bf16[16,6,768]{2,1,0:T(8,128)(2,1)S(1)} %get-tuple-element.54), channel_id=1, source_target_pairs={{0,1},{1,2},{2,3},{3,4},{4,5},{5,6},{6,7},{7,8},{8,9},{9,10},{10,1... | collective-permute-start | bytes 442376 | tf_op jit(solution)/shard_map/ppermute | solution.py:32
  168.2 1.3 collective-permute-start.5
  169.5 1.6 select_maximum_fusion.small
  171.1 0.0 copy-start
  171.1 80.4 %shard_map.148 = (f32[2,4,48,768]{3,2,1,0:T(8,128)}, f32[56,768]{1,0:T(8,128)}) custom-call(bf16[4,4,2,2,48,768]{5,4,3,2,1,0:T(8,128)(2,1)} %bitcast.34, bf16[4,2,2,4,48,768]{5,4,3,2,1,0:T(8,128)(2,1)} %bitcast.35, f32[56,768]{1,0:T(8,128)} %select_maximum_fusion.small), custom_call_target="tpu_custom_call" | custom-call | tf_op jit(solution)/shard_map/pallas_call | solution.py:577
  251.5 2.2 slice_multiply_fusion
  253.6 0.9 copy.21
  254.5 0.0 collective-permute-done.4
  254.5 0.0 collective-permute-done.5
  254.5 0.0 copy-done
  254.5 0.3 pad_maximum_fusion.4
  254.8 2.3 collective-permute-start.6
  257.2 1.3 collective-permute-start.7
  258.5 0.9 multiply_bitcast_fusion.1
  259.4 0.7 copy.19
  260.1 0.7 slice_multiply_fusion.1
  260.8 0.6 mul.72
  261.4 1.4 multiply_reduce_fusion
  262.8 0.0 collective-permute-done.6
  262.8 0.0 collective-permute-done.7
  262.8 1.9 pad_maximum_fusion.1.padded_ref
  264.7 11.5 %shard_map.146 = bf16[16,32,768]{2,1,0:T(8,128)(2,1)} custom-call(bf16[28,44,768]{2,1,0:T(8,128)(2,1)} %pad_maximum_fusion.1.padded_ref, f32[49,768]{1,0:T(8,128)} %rev.3.taps_ref, bf16[16,32,768]{2,1,0:T(8,128)(2,1)} %cot_ref.1), custom_call_target="tpu_custom_call" | custom-call | flops 38535168 | bytes 3145728 | tf_op jit(solution)/shard_map/pallas_call | solution.py:123
  (1 shorter events, 0.0 us)
Async XLA Ops:
  0.6 103.0 %copy-start.1 = (bf16[16,32,768]{2,1,0:T(8,128)(2,1)S(1)}, bf16[16,32,768]{2,1,0:T(8,128)(2,1)}, u32[]{:S(2)}) copy-start(bf16[16,32,768]{2,1,0:T(8,128)(2,1)} %param.8) | copy-start | bytes 2359300
  1.8 9.0 %collective-permute-start = (bf16[16,6,768]{2,1,0:T(8,128)(2,1)S(1)}, bf16[16,6,768]{2,1,0:T(8,128)(2,1)S(1)}, u32[]{:S(2)}, u32[]{:S(2)}) collective-permute-start(bf16[16,6,768]{2,1,0:T(8,128)(2,1)S(1)} %get-tuple-element.56), channel_id=1, source_target_pairs={{0,1},{1,2},{2,3},{3,4},{4,5},{5,6},{6,7},{7,8},{8,9},{9,10},{10,1... | collective-permute-start | bytes 442376 | tf_op jit(solution)/shard_map/ppermute | solution.py:32
  6.7 10.3 %collective-permute-start.1 = (bf16[16,6,768]{2,1,0:T(8,128)(2,1)S(1)}, bf16[16,6,768]{2,1,0:T(8,128)(2,1)S(1)}, u32[]{:S(2)}, u32[]{:S(2)}) collective-permute-start(bf16[16,6,768]{2,1,0:T(8,128)(2,1)S(1)} %get-tuple-element.57), channel_id=1, source_target_pairs={{1,0},{2,1},{3,2},{4,3},{5,4},{6,5},{7,6},{8,7},{9,8},{10,9},{11,1... | collective-permute-start | bytes 442376 | tf_op jit(solution)/shard_map/ppermute | solution.py:33
  18.3 85.3 %collective-permute-start.2 = (bf16[6,44,768]{2,1,0:T(8,128)(2,1)S(1)}, bf16[6,44,768]{2,1,0:T(8,128)(2,1)S(1)}, u32[]{:S(2)}, u32[]{:S(2)}) collective-permute-start(bf16[6,44,768]{2,1,0:T(8,128)(2,1)S(1)} %get-tuple-element.52), channel_id=1, source_target_pairs={{0,16},{1,17},{2,18},{3,19},{4,20},{5,21},{6,22},{7,23},{8,24},{9,... | collective-permute-start | bytes 1216520 | tf_op jit(solution)/shard_map/ppermute | solution.py:35
  19.6 84.0 %collective-permute-start.3 = (bf16[6,44,768]{2,1,0:T(8,128)(2,1)S(1)}, bf16[6,44,768]{2,1,0:T(8,128)(2,1)S(1)}, u32[]{:S(2)}, u32[]{:S(2)}) collective-permute-start(bf16[6,44,768]{2,1,0:T(8,128)(2,1)S(1)} %get-tuple-element.53), channel_id=1, source_target_pairs={{16,0},{17,1},{18,2},{19,3},{20,4},{21,5},{22,6},{23,7},{24,8},{25... | collective-permute-start | bytes 1216520 | tf_op jit(solution)/shard_map/ppermute | solution.py:36
  164.8 89.7 %collective-permute-start.4 = (bf16[16,6,768]{2,1,0:T(8,128)(2,1)S(1)}, bf16[16,6,768]{2,1,0:T(8,128)(2,1)S(1)}, u32[]{:S(2)}, u32[]{:S(2)}) collective-permute-start(bf16[16,6,768]{2,1,0:T(8,128)(2,1)S(1)} %get-tuple-element.54), channel_id=1, source_target_pairs={{0,1},{1,2},{2,3},{3,4},{4,5},{5,6},{6,7},{7,8},{8,9},{9,10},{10,1... | collective-permute-start | bytes 442376 | tf_op jit(solution)/shard_map/ppermute | solution.py:32
  168.2 86.3 %collective-permute-start.5 = (bf16[16,6,768]{2,1,0:T(8,128)(2,1)S(1)}, bf16[16,6,768]{2,1,0:T(8,128)(2,1)S(1)}, u32[]{:S(2)}, u32[]{:S(2)}) collective-permute-start(bf16[16,6,768]{2,1,0:T(8,128)(2,1)S(1)} %get-tuple-element.55), channel_id=1, source_target_pairs={{1,0},{2,1},{3,2},{4,3},{5,4},{6,5},{7,6},{8,7},{9,8},{10,9},{11,1... | collective-permute-start | bytes 442376 | tf_op jit(solution)/shard_map/ppermute | solution.py:33
  171.1 83.4 %copy-start = (bf16[512,768]{1,0:T(8,128)(2,1)S(1)}, bf16[512,768]{1,0:T(8,128)(2,1)}, u32[]{:S(2)}) copy-start(bf16[512,768]{1,0:T(8,128)(2,1)} %get-tuple-element.22) | copy-start | bytes 2359300
  254.8 8.0 %collective-permute-start.6 = (bf16[6,44,768]{2,1,0:T(8,128)(2,1)S(1)}, bf16[6,44,768]{2,1,0:T(8,128)(2,1)S(1)}, u32[]{:S(2)}, u32[]{:S(2)}) collective-permute-start(bf16[6,44,768]{2,1,0:T(8,128)(2,1)S(1)} %get-tuple-element.50), channel_id=1, source_target_pairs={{0,16},{1,17},{2,18},{3,19},{4,20},{5,21},{6,22},{7,23},{8,24},{9,... | collective-permute-start | bytes 1216520 | tf_op jit(solution)/shard_map/ppermute | solution.py:35
  257.2 5.7 %collective-permute-start.7 = (bf16[6,44,768]{2,1,0:T(8,128)(2,1)S(1)}, bf16[6,44,768]{2,1,0:T(8,128)(2,1)S(1)}, u32[]{:S(2)}, u32[]{:S(2)}) collective-permute-start(bf16[6,44,768]{2,1,0:T(8,128)(2,1)S(1)} %get-tuple-element.51), channel_id=1, source_target_pairs={{16,0},{17,1},{18,2},{19,3},{20,4},{21,5},{22,6},{23,7},{24,8},{25... | collective-permute-start | bytes 1216520 | tf_op jit(solution)/shard_map/ppermute | solution.py:36

commit v3 on v2

--- a/solution.py
+++ b/solution.py
@@ -70,7 +70,7 @@
     lax.fori_loop(0, 2 * PHASES, block, 0)
 
 
-def forward_kernel(padded_ref, taps_ref, out_ref, flat, phased, summed):
+def forward_block(padded_ref, taps_ref, out_ref, flat, phased, summed):
     spread(padded_ref, flat, phased, 4 * PHASES)
     stencil_blocks(taps_ref, phased, summed, out_ref.shape[0] // 2)
     out_ref[...] = summed[...].astype(jnp.bfloat16)
@@ -360,7 +360,10 @@
             copy.wait_send()
 
 
-def gather_kernel(shard_in, shard_out, full_in, full_out, send_sems, recv_sems, own_sems):
+def gather_kernel(
+    shard_in, shard_out, padded_ref, taps_ref, full_in, full_out, conv_ref,
+    send_sems, recv_sems, own_sems, flat, phased, summed,
+):
     place = Place()
     z, y, x = place.z, place.y, place.x
     mine = pl.ds(2 * place.core, 2)
@@ -399,18 +402,25 @@
 
     pieces = [(array, part) for array in range(2) for part in range(PARTS)]
     flying = [[] for _ in pieces]
-    for tick in range(len(pieces) + 4):
-        for index in range(len(pieces) - 1, -1, -1):
-            stage = tick - index
+    blocks = list(range(0, conv_ref.shape[2], LANES))
+    for tick in range(len(pieces) // PARTS + 4):
+        for index in range(len(pieces)):
+            stage = tick - index // PARTS
             if 0 <= stage <= 4:
                 for copy in flying[index]:
                     copy.wait_recv()
                 if stage < 4:
                     flying[index] = send(pieces[index], stage)
+        for start in blocks[2 * tick : 2 * tick + 2]:
+            lanes = pl.ds(start, LANES)
+            forward_block(
+                padded_ref.at[:, :, lanes], taps_ref.at[:, lanes], conv_ref.at[:, :, lanes],
+                flat, phased, summed,
+            )
     mail.finish()
 
 
-def gather_call(w_in, w_out):
+def gather_call(w_in, w_out, padded, taps, tile_shape):
     depth = lax.axis_size("col") // 4
     in_rows, hidden_units = w_in.shape
     out_rows, channels = w_out.shape
@@ -419,24 +429,31 @@
     shard_out = w_out.reshape(4, height, channels)
     copies = 4 * (depth - 1 + 3)
     anywhere = pl.BlockSpec(memory_space=pl.ANY)
-    full_in, full_out = pl.pallas_call(
+    vmem = pl.BlockSpec(memory_space=pltpu.VMEM)
+    padded_rows, padded_cols, _ = padded.shape
+    full_in, full_out, conv = pl.pallas_call(
         gather_kernel,
         out_shape=(
             jax.ShapeDtypeStruct((4, depth, 2, 2, in_rows, width), w_in.dtype),
             jax.ShapeDtypeStruct((depth, 2, 2, 4, height, channels), w_out.dtype),
+            jax.ShapeDtypeStruct(tile_shape, jnp.bfloat16),
         ),
-        in_specs=[anywhere, anywhere],
-        out_specs=(anywhere, anywhere),
+        in_specs=[anywhere, anywhere, vmem, vmem],
+        out_specs=(anywhere, anywhere, vmem),
         scratch_shapes=[
             pltpu.SemaphoreType.DMA((copies,)),
             pltpu.SemaphoreType.DMA((copies,)),
             pltpu.SemaphoreType.DMA((2,)),
+            pltpu.VMEM((padded_rows, padded_cols, LANES), jnp.float32),
+            pltpu.VMEM((padded_rows, 4 * PHASES, 8, LANES), jnp.float32),
+            pltpu.VMEM(tile_shape[:2] + (LANES,), jnp.float32),
         ],
         compiler_params=pltpu.CompilerParams(
             collective_id=0, has_side_effects=True, vmem_limit_bytes=VMEM_BYTES
         ),
-    )(shard_in, shard_out)
-    return full_in.reshape(4, 4 * depth * in_rows, width), full_out.reshape(-1, channels)
+    )(shard_in, shard_out, padded, taps)
+    full_in = full_in.reshape(4, 4 * depth * in_rows, width)
+    return full_in, full_out.reshape(-1, channels), conv
 
 
 def scatter_kernel(
@@ -555,10 +572,10 @@
         return []
 
     small_flying = [small_copy]
-    for tick in range(len(pieces) + 4):
-        for index in range(len(pieces) - 1, -1, -1):
-            if 0 <= tick - index <= 4:
-                flying[index] = advance(index, tick - index)
+    for tick in range(len(pieces) // PARTS + 4):
+        for index in range(len(pieces)):
+            if 0 <= tick - index // PARTS <= 4:
+                flying[index] = advance(index, tick - index // PARTS)
         if tick < 4:
             small_flying = advance_small(tick)
     mail.finish()
@@ -608,10 +625,9 @@
     pixels = tile_rows * tile_cols
     scale_factor = 1.0 / math.sqrt(pixels * group_count)
     flat = lambda field: field.reshape(pixels, channels)
-    full_in, full_out = gather_call(w_in, w_out)
     taps = dw_kernel.T
     padded = halo_pad(image)
-    conv = stencil_call(forward_kernel, padded, taps, (), tile_shape)
+    full_in, full_out, conv = gather_call(w_in, w_out, padded, taps, tile_shape)
     out_map, grad_conv, grad_in, grad_out, bias_part, gain_part, scale_part = mlp_call(
         flat(conv),
         flat(image),

time: 279 us -> 271 us (0.971)
  Pallas kernels: 223 us -> 218 us
    pallas_call x2 -> x1, Pallas kernels: 22.8 us -> 11.5 us  [stencil_call(): pl.pallas_call(kernel, grid=(channels // LANES,), out_shape=jax.ShapeDtyp...]
    pallas_call x1, Pallas kernels: 75 us -> 78.1 us  [gather_call(): pl.pallas_call(gather_kernel, out_shape=(jax.ShapeDtypeStruct((4, depth,...]
  transfers between devices with their start and end apart: 8 -> 8, of which waited for: 2 -> 2; matrix products, arithmetic and copies ran while one was open for 6% -> 6% of each run, Pallas kernels for 56% -> 31%
where the time goes in v3:
time: 271 us; the launch traced here: 269 us
  Pallas kernels  218 us (80%)
  starting transfers between devices  15 us (6%)
  other arithmetic  13.5 us (5%)
  local copies, waits for them, and re-layouts  12.6 us (5%)
  waiting for transfers between devices  9.01 us (3%)
    pallas_call x1, Pallas kernels, scatter_call(): pl.pallas_call(scatter_kernel, out_shape=(jax.ShapeDtypeStruct((2, 4, hei...  83 us
    pallas_call x1, Pallas kernels, gather_call(): pl.pallas_call(gather_kernel, out_shape=(jax.ShapeDtypeStruct((4, depth,...  78.1 us
    pallas_call x1, Pallas kernels, mlp_call(): pl.pallas_call(mlp_kernel, grid=(hidden_units // chunk,), out_shape=(bf16...  34.6 us
    pallas_call x1, Pallas kernels, stencil_call(): pl.pallas_call(kernel, grid=(channels // LANES,), out_shape=jax.ShapeDtyp...  11.5 us
    pallas_call x1, Pallas kernels, taps_call(): pl.pallas_call(taps_kernel, grid=(channels // LANES,), out_shape=jax.Shap...  10.5 us
    ppermute x2, waiting for transfers between devices, halo_pad(): right = lax.ppermute(tile[:, :REACH], 'col', back(cols))  6.16 us
    ppermute x2, starting transfers between devices, halo_pad(): left = lax.ppermute(tile[:, -REACH:], 'col', ahead(cols))  6.16 us
  transfers between devices with their start and end apart: 8, of which 2 were waited for; matrix products, arithmetic and copies ran while one was open for 6% of the time, Pallas kernels for 31%

profile of v3, /device:TPU:0, one launch (start us, length us, event | category | flops | bytes accessed | tf_op | source)
XLA Modules:
  0.0 268.7 jit_solution(11905852868011842522)
XLA Ops:
  0.6 0.0 copy-start.1
  0.6 1.1 fusion.1
  1.8 4.9 %collective-permute-start = (bf16[16,6,768]{2,1,0:T(8,128)(2,1)S(1)}, bf16[16,6,768]{2,1,0:T(8,128)(2,1)S(1)}, u32[]{:S(2)}, u32[]{:S(2)}) collective-permute-start(bf16[16,6,768]{2,1,0:T(8,128)(2,1)S(1)} %get-tuple-element.58), channel_id=1, source_target_pairs={{0,1},{1,2},{2,3},{3,4},{4,5},{5,6},{6,7},{7,8},{8,9},{9,10},{10,1... | collective-permute-start | bytes 442376 | tf_op jit(solution)/shard_map/ppermute | solution.py:32
  6.7 1.3 collective-permute-start.1
  8.0 2.8 %collective-permute-done = bf16[16,6,768]{2,1,0:T(8,128)(2,1)S(1)} collective-permute-done((bf16[16,6,768]{2,1,0:T(8,128)(2,1)S(1)}, bf16[16,6,768]{2,1,0:T(8,128)(2,1)S(1)}, u32[]{:S(2)}, u32[]{:S(2)}) %collective-permute-start) | collective-permute-done | bytes 147488 | tf_op jit(solution)/shard_map/ppermute | solution.py:32
  10.8 6.2 %collective-permute-done.1 = bf16[16,6,768]{2,1,0:T(8,128)(2,1)S(1)} collective-permute-done((bf16[16,6,768]{2,1,0:T(8,128)(2,1)S(1)}, bf16[16,6,768]{2,1,0:T(8,128)(2,1)S(1)}, u32[]{:S(2)}, u32[]{:S(2)}) %collective-permute-start.1) | collective-permute-done | bytes 147488 | tf_op jit(solution)/shard_map/ppermute | solution.py:33
  16.9 1.3 pad_maximum_fusion.7
  18.3 1.3 collective-permute-start.2
  19.6 1.3 collective-permute-start.3
  20.9 1.7 copy.23
  22.6 1.3 broadcast_in_dim.10.layer_ref
  23.9 1.3 broadcast_in_dim.9.gain_ref
  25.1 3.5 %rev.3.taps_ref = f32[49,768]{1,0:T(8,128)} reverse(f32[49,768]{1,0:T(8,128)} %bitcast.38), dimensions={0} | reverse | bytes 301056 | tf_op jit(solution)/shard_map/rev | solution.py:645
  28.7 0.0 collective-permute-done.2
  28.7 0.0 collective-permute-done.3
  28.7 0.0 copy-done.1
  28.7 1.8 pad_maximum_fusion.padded_ref
  30.5 78.1 %shard_map.143 = (bf16[4,4,2,2,48,768]{5,4,3,2,1,0:T(8,128)(2,1)}, bf16[4,2,2,4,48,768]{5,4,3,2,1,0:T(8,128)(2,1)}, bf16[16,32,768]{2,1,0:T(8,128)(2,1)}) custom-call(bf16[4,48,768]{2,1,0:T(8,128)(2,1)} %bitcast.36, bf16[4,48,768]{2,1,0:T(8,128)(2,1)} %bitcast.43, bf16[28,44,768]{2,1,0:T(8,128)(2,1)} %pad_maximum_fusion.padded_ref, f32[49,768]{1,0:T(8,128)} %bitcast.39), custom_call_target="tpu_custom_call" | custom-call | tf_op jit(solution)/shard_map/pallas_call | solution.py:434
  108.6 34.6 %shard_map.144 = (bf16[512,768]{1,0:T(8,128)(2,1)}, bf16[512,768]{1,0:T(8,128)(2,1)}, bf16[4,768,768]{2,1,0:T(8,128)(2,1)}, bf16[3072,768]{1,0:T(8,128)(2,1)}, f...) custom-call(bf16[512,768]{1,0:T(8,128)(2,1)} %bitcast.47, bf16[512,768]{1,0:T(8,128)(2,1)} %bitcast.33, ...), custom_call_target="tpu_custom_call" | custom-call | flops 14495514624 | bytes 28311552 | tf_op jit(solution)/shard_map/pallas_call | solution.py:253
  143.2 10.5 %shard_map.146 = f32[49,768]{1,0:T(8,128)} custom-call(bf16[28,44,768]{2,1,0:T(8,128)(2,1)} %pad_maximum_fusion.padded_ref, bf16[16,32,768]{2,1,0:T(8,128)(2,1)} %bitcast.29), custom_call_target="tpu_custom_call" | custom-call | flops 38535168 | bytes 3145728 | tf_op jit(solution)/shard_map/pallas_call | solution.py:147
  153.7 1.1 fusion
  154.7 0.5 broadcast.38
  155.3 1.4 reduce.7
  156.7 1.3 collective-permute-start.4
  158.0 1.3 collective-permute-start.5
  159.3 1.6 select_maximum_fusion.small
  160.9 0.0 copy-start
  160.9 83.0 %shard_map.147 = (f32[2,4,48,768]{3,2,1,0:T(8,128)}, f32[56,768]{1,0:T(8,128)}) custom-call(bf16[4,4,2,2,48,768]{5,4,3,2,1,0:T(8,128)(2,1)} %bitcast.34, bf16[4,2,2,4,48,768]{5,4,3,2,1,0:T(8,128)(2,1)} %bitcast.35, f32[56,768]{1,0:T(8,128)} %select_maximum_fusion.small), custom_call_target="tpu_custom_call" | custom-call | tf_op jit(solution)/shard_map/pallas_call | solution.py:594
  243.9 2.2 slice_multiply_fusion
  246.1 0.9 copy.21
  247.0 0.0 collective-permute-done.4
  247.0 0.0 collective-permute-done.5
  247.0 0.0 copy-done
  247.0 0.3 pad_maximum_fusion.4
  247.3 2.3 collective-permute-start.6
  249.6 1.3 collective-permute-start.7
  250.9 0.9 multiply_bitcast_fusion.1
  251.8 0.7 copy.19
  252.5 0.7 slice_multiply_fusion.1
  253.3 0.6 mul.72
  253.9 1.4 multiply_reduce_fusion
  255.3 0.0 collective-permute-done.6
  255.3 0.0 collective-permute-done.7
  255.3 1.9 pad_maximum_fusion.1.padded_ref
  257.2 11.5 %shard_map.145 = bf16[16,32,768]{2,1,0:T(8,128)(2,1)} custom-call(bf16[28,44,768]{2,1,0:T(8,128)(2,1)} %pad_maximum_fusion.1.padded_ref, f32[49,768]{1,0:T(8,128)} %rev.3.taps_ref, bf16[16,32,768]{2,1,0:T(8,128)(2,1)} %cot_ref.1), custom_call_target="tpu_custom_call" | custom-call | flops 38535168 | bytes 3145728 | tf_op jit(solution)/shard_map/pallas_call | solution.py:123
  (1 shorter events, 0.0 us)
Async XLA Ops:
  0.6 28.0 %copy-start.1 = (bf16[16,32,768]{2,1,0:T(8,128)(2,1)S(1)}, bf16[16,32,768]{2,1,0:T(8,128)(2,1)}, u32[]{:S(2)}) copy-start(bf16[16,32,768]{2,1,0:T(8,128)(2,1)} %param.8) | copy-start | bytes 2359300
  1.8 9.0 %collective-permute-start = (bf16[16,6,768]{2,1,0:T(8,128)(2,1)S(1)}, bf16[16,6,768]{2,1,0:T(8,128)(2,1)S(1)}, u32[]{:S(2)}, u32[]{:S(2)}) collective-permute-start(bf16[16,6,768]{2,1,0:T(8,128)(2,1)S(1)} %get-tuple-element.58), channel_id=1, source_target_pairs={{0,1},{1,2},{2,3},{3,4},{4,5},{5,6},{6,7},{7,8},{8,9},{9,10},{10,1... | collective-permute-start | bytes 442376 | tf_op jit(solution)/shard_map/ppermute | solution.py:32
  6.7 10.3 %collective-permute-start.1 = (bf16[16,6,768]{2,1,0:T(8,128)(2,1)S(1)}, bf16[16,6,768]{2,1,0:T(8,128)(2,1)S(1)}, u32[]{:S(2)}, u32[]{:S(2)}) collective-permute-start(bf16[16,6,768]{2,1,0:T(8,128)(2,1)S(1)} %get-tuple-element.59), channel_id=1, source_target_pairs={{1,0},{2,1},{3,2},{4,3},{5,4},{6,5},{7,6},{8,7},{9,8},{10,9},{11,1... | collective-permute-start | bytes 442376 | tf_op jit(solution)/shard_map/ppermute | solution.py:33
  18.3 10.4 %collective-permute-start.2 = (bf16[6,44,768]{2,1,0:T(8,128)(2,1)S(1)}, bf16[6,44,768]{2,1,0:T(8,128)(2,1)S(1)}, u32[]{:S(2)}, u32[]{:S(2)}) collective-permute-start(bf16[6,44,768]{2,1,0:T(8,128)(2,1)S(1)} %get-tuple-element.54), channel_id=1, source_target_pairs={{0,16},{1,17},{2,18},{3,19},{4,20},{5,21},{6,22},{7,23},{8,24},{9,... | collective-permute-start | bytes 1216520 | tf_op jit(solution)/shard_map/ppermute | solution.py:35
  19.6 9.0 %collective-permute-start.3 = (bf16[6,44,768]{2,1,0:T(8,128)(2,1)S(1)}, bf16[6,44,768]{2,1,0:T(8,128)(2,1)S(1)}, u32[]{:S(2)}, u32[]{:S(2)}) collective-permute-start(bf16[6,44,768]{2,1,0:T(8,128)(2,1)S(1)} %get-tuple-element.55), channel_id=1, source_target_pairs={{16,0},{17,1},{18,2},{19,3},{20,4},{21,5},{22,6},{23,7},{24,8},{25... | collective-permute-start | bytes 1216520 | tf_op jit(solution)/shard_map/ppermute | solution.py:36
  156.7 90.3 %collective-permute-start.4 = (bf16[16,6,768]{2,1,0:T(8,128)(2,1)S(1)}, bf16[16,6,768]{2,1,0:T(8,128)(2,1)S(1)}, u32[]{:S(2)}, u32[]{:S(2)}) collective-permute-start(bf16[16,6,768]{2,1,0:T(8,128)(2,1)S(1)} %get-tuple-element.56), channel_id=1, source_target_pairs={{0,1},{1,2},{2,3},{3,4},{4,5},{5,6},{6,7},{7,8},{8,9},{9,10},{10,1... | collective-permute-start | bytes 442376 | tf_op jit(solution)/shard_map/ppermute | solution.py:32
  158.0 89.0 %collective-permute-start.5 = (bf16[16,6,768]{2,1,0:T(8,128)(2,1)S(1)}, bf16[16,6,768]{2,1,0:T(8,128)(2,1)S(1)}, u32[]{:S(2)}, u32[]{:S(2)}) collective-permute-start(bf16[16,6,768]{2,1,0:T(8,128)(2,1)S(1)} %get-tuple-element.57), channel_id=1, source_target_pairs={{1,0},{2,1},{3,2},{4,3},{5,4},{6,5},{7,6},{8,7},{9,8},{10,9},{11,1... | collective-permute-start | bytes 442376 | tf_op jit(solution)/shard_map/ppermute | solution.py:33
  160.9 86.1 %copy-start = (bf16[512,768]{1,0:T(8,128)(2,1)S(1)}, bf16[512,768]{1,0:T(8,128)(2,1)}, u32[]{:S(2)}) copy-start(bf16[512,768]{1,0:T(8,128)(2,1)} %get-tuple-element.24) | copy-start | bytes 2359300
  247.3 8.0 %collective-permute-start.6 = (bf16[6,44,768]{2,1,0:T(8,128)(2,1)S(1)}, bf16[6,44,768]{2,1,0:T(8,128)(2,1)S(1)}, u32[]{:S(2)}, u32[]{:S(2)}) collective-permute-start(bf16[6,44,768]{2,1,0:T(8,128)(2,1)S(1)} %get-tuple-element.52), channel_id=1, source_target_pairs={{0,16},{1,17},{2,18},{3,19},{4,20},{5,21},{6,22},{7,23},{8,24},{9,... | collective-permute-start | bytes 1216520 | tf_op jit(solution)/shard_map/ppermute | solution.py:35
  249.6 5.7 %collective-permute-start.7 = (bf16[6,44,768]{2,1,0:T(8,128)(2,1)S(1)}, bf16[6,44,768]{2,1,0:T(8,128)(2,1)S(1)}, u32[]{:S(2)}, u32[]{:S(2)}) collective-permute-start(bf16[6,44,768]{2,1,0:T(8,128)(2,1)S(1)} %get-tuple-element.53), channel_id=1, source_target_pairs={{16,0},{17,1},{18,2},{19,3},{20,4},{21,5},{22,6},{23,7},{24,8},{25... | collective-permute-start | bytes 1216520 | tf_op jit(solution)/shard_map/ppermute | solution.py:36
